TPU v7x, 32 devices: a whole 2x2x4 slice. The times are simulated.
32 devices in a mesh: dp: 16 (over z, y, core), tensor: 2 (over x).
Axes of the slice: x: 2, y: 2, z: 4, core: 2. Of those that a mesh axis runs over, the one named last changes fastest.
Arguments:
- block_input: bfloat16 [18688, 1024], P(('dp', 'tensor')), may hold values from -6 to 6
- image_mask: int32 [32], P('dp'), may hold values 0 or 1
- w_qkv: bfloat16 [3, 1024, 1024], P(None, 'dp', 'tensor'), may hold values from -0.1875 to 0.1875
- b_qv: float32 [2, 1024], P(None, 'tensor'), may hold values from -1.5 to 1.5
- w_out: bfloat16 [1024, 1024], P('tensor', 'dp'), may hold values from -1.5 to 1.5
- b_out: float32 [1024], replicated, may hold values from -1.5 to 1.5
- w_fc1: bfloat16 [1024, 4096], P('dp', 'tensor'), may hold values from -0.1875 to 0.1875
- b_fc1: float32 [4096], P('tensor'), may hold values from -1.5 to 1.5
- w_fc2: bfloat16 [4096, 1024], P('tensor', 'dp'), may hold values from -0.09375 to 0.09375
- b_fc2: float32 [1024], replicated, may hold values from -1.5 to 1.5
- ln1_gain: float32 [1024], replicated, may hold values from 0.5 to 1.5
- ln1_bias: float32 [1024], replicated, may hold values from -1.5 to 1.5
- ln2_gain: float32 [1024], replicated, may hold values from 0.5 to 1.5
- ln2_bias: float32 [1024], replicated, may hold values from -1.5 to 1.5
- grad_out: bfloat16 [18688, 1024], P(('dp', 'tensor')), may hold values from -6 to 6
Outputs:
- layer_output: bfloat16 [18688, 1024], P(('dp', 'tensor'))
- input_grad: bfloat16 [18688, 1024], P(('dp', 'tensor'))
- grad_w_qkv: float32 [3, 1024, 1024], P(None, 'dp', 'tensor')
- grad_b_qv: float32 [2, 1024], P(None, 'tensor')
- grad_w_out: float32 [1024, 1024], P('tensor', 'dp')
- grad_b_out: float32 [1024], replicated
- grad_w_fc1: float32 [1024, 4096], P('dp', 'tensor')
- grad_b_fc1: float32 [4096], P('tensor')
- grad_w_fc2: float32 [4096, 1024], P('tensor', 'dp')
- grad_b_fc2: float32 [1024], replicated
- grad_ln1_gain: float32 [1024], replicated
- grad_ln1_bias: float32 [1024], replicated
- grad_ln2_gain: float32 [1024], replicated
- grad_ln2_bias: float32 [1024], replicated
All inputs are finite; a program needn't handle non-finite values. No bound on the sum of `image_mask` on one device may be relied on, other than what follows from the above.
Results may differ from a plain program's by a relative error of at most 0.0098.
Values may be sent and summed in bfloat16 or wider, within the bound.
No kernel may reach another device: no remote copies, remote signals or barrier semaphores. Data moves between devices by JAX's collectives and lax.ppermute only.
A program may use at most 128 MiB of HBM per device.

v0:
```python
import jax
import jax.numpy as jnp
from jax import lax
from jax.sharding import PartitionSpec as P

HEADS = 16
SEQ = 584
VALID = 577


layer_eps = 1e-06
masked_score = -1e30


def normalize(signal, gain_vec, bias_vec):
    row_mean = jnp.mean(signal, axis=-1, keepdims=True)
    centred = signal - row_mean
    row_spread = jnp.mean(centred * centred, axis=-1, keepdims=True)
    return centred * lax.rsqrt(row_spread + layer_eps) * gain_vec + bias_vec


def gelu_exact(signal):
    return jax.nn.gelu(signal, approximate=False)


def masked_scores(queries, key_proj):
    score_scale = queries.shape[-1] ** (-0.5)
    scores = (
        jnp.einsum("qhe,khe->hqk", queries, key_proj, preferred_element_type=jnp.float32)
        * score_scale
    )
    valid_keys = jnp.arange(scores.shape[-1]) < VALID
    return jnp.where(valid_keys[None, None, :], scores, masked_score)


def attend_image(operands):
    queries, key_proj, value_proj = operands
    logits = masked_scores(queries, key_proj)
    row_top = jnp.max(logits, axis=-1, keepdims=True)
    row_expo = jnp.exp(logits - row_top)
    row_total = jnp.sum(row_expo, axis=-1, keepdims=True)
    weights = (row_expo / row_total).astype(jnp.bfloat16)
    head_mixed = jnp.einsum("hqk,khe->qhe", weights, value_proj, preferred_element_type=jnp.float32)
    return (head_mixed.astype(jnp.bfloat16), (row_top + jnp.log(row_total))[..., 0])


def attend_back(operands):
    queries, key_proj, value_proj, mixed_grad, row_lse = operands
    score_scale = queries.shape[-1] ** (-0.5)
    logits = masked_scores(queries, key_proj)
    probs = jnp.exp(logits - row_lse[..., None])
    value_grad = jnp.einsum(
        "hqk,qhe->khe", probs.astype(jnp.bfloat16), mixed_grad, preferred_element_type=jnp.float32
    )
    prob_grad = jnp.einsum(
        "qhe,khe->hqk", mixed_grad, value_proj, preferred_element_type=jnp.float32
    )
    score_grad = probs * (prob_grad - jnp.sum(probs * prob_grad, axis=-1, keepdims=True))
    score_grad = score_grad.astype(jnp.bfloat16)
    query_grad = (
        jnp.einsum("hqk,khe->qhe", score_grad, key_proj, preferred_element_type=jnp.float32)
        * score_scale
    )
    key_grad = (
        jnp.einsum("hqk,qhe->khe", score_grad, queries, preferred_element_type=jnp.float32)
        * score_scale
    )
    return (
        query_grad.astype(jnp.bfloat16),
        key_grad.astype(jnp.bfloat16),
        value_grad.astype(jnp.bfloat16),
    )


def local(
    block_input,
    image_mask,
    w_qkv,
    b_qv,
    w_out,
    b_out,
    w_fc1,
    b_fc1,
    w_fc2,
    b_fc2,
    ln1_gain,
    ln1_bias,
    ln2_gain,
    ln2_bias,
    grad_out,
):
    local_rows = block_input.shape[0]
    model_width = block_input.shape[1]
    image_count = image_mask.shape[0]
    head_dim = model_width // HEADS
    local_width = w_qkv.shape[2]
    local_heads = local_width // head_dim
    tensor_index = lax.axis_index("tensor")
    token_index = tensor_index * local_rows + jnp.arange(local_rows)
    image_of = token_index // SEQ
    position = token_index % SEQ
    image_pick = (image_of[:, None] == jnp.arange(image_count)[None, :]).astype(jnp.float32)
    token_keep = jnp.sum(image_pick * image_mask.astype(jnp.float32)[None, :], axis=1)
    token_keep = token_keep * (position < VALID).astype(jnp.float32)
    contract_rows = (((0,), (0,)), ((), ()))
    contract_cols = (((1,), (1,)), ((), ()))
    full_qkv, full_out, full_fc1, full_fc2 = (
        lax.all_gather(w_qkv, "dp", axis=1, tiled=True),
        lax.all_gather(w_out, "dp", axis=1, tiled=True),
        lax.all_gather(w_fc1, "dp", axis=0, tiled=True),
        lax.all_gather(w_fc2, "dp", axis=1, tiled=True),
    )
    input_float = block_input.astype(jnp.float32)
    normed_one = normalize(input_float, ln1_gain, ln1_bias).astype(jnp.bfloat16)
    inputs_one = lax.all_gather(normed_one, "tensor", axis=0, tiled=True)
    group_rows = inputs_one.shape[0]
    projected = jnp.einsum("td,cde->cte", inputs_one, full_qkv, preferred_element_type=jnp.float32)
    queries = (projected[0] + b_qv[0]).astype(jnp.bfloat16)
    key_proj = projected[1].astype(jnp.bfloat16)
    value_proj = (projected[2] + b_qv[1]).astype(jnp.bfloat16)
    head_shape = (group_rows // SEQ, SEQ, local_heads, head_dim)
    query_heads = queries.reshape(head_shape)
    key_heads = key_proj.reshape(head_shape)
    value_heads = value_proj.reshape(head_shape)
    head_mixed, row_lse = lax.map(attend_image, (query_heads, key_heads, value_heads))
    head_mixed = head_mixed.reshape(group_rows, local_width)
    row_block = head_mixed
    attn_sum = lax.psum_scatter(
        jnp.dot(row_block, full_out, preferred_element_type=jnp.float32),
        "tensor",
        scatter_dimension=0,
        tiled=True,
    )
    resid = input_float + (attn_sum + b_out)
    normed_two = normalize(resid, ln2_gain, ln2_bias).astype(jnp.bfloat16)
    inputs_two = lax.all_gather(normed_two, "tensor", axis=0, tiled=True)
    hidden_pre = jnp.dot(inputs_two, full_fc1, preferred_element_type=jnp.float32) + b_fc1
    hidden = gelu_exact(hidden_pre).astype(jnp.bfloat16)
    row_block = hidden
    mlp_sum = lax.psum_scatter(
        jnp.dot(row_block, full_fc2, preferred_element_type=jnp.float32).astype(jnp.bfloat16),
        "tensor",
        scatter_dimension=0,
        tiled=True,
    ).astype(jnp.float32)
    layer_output = ((resid + (mlp_sum + b_fc2)) * token_keep[:, None]).astype(jnp.bfloat16)
    cot_rows = grad_out * token_keep.astype(jnp.bfloat16)[:, None]
    cot_float = cot_rows.astype(jnp.float32)
    cot_group = lax.all_gather(cot_rows, "tensor", axis=0, tiled=True)
    fc2_grad_group = lax.dot_general(
        hidden, cot_group, contract_rows, preferred_element_type=jnp.float32
    )
    hidden_grad = lax.dot_general(
        cot_group, full_fc2, contract_cols, preferred_element_type=jnp.float32
    )
    gelu_value, gelu_back = jax.vjp(gelu_exact, hidden_pre)
    pre_grad = gelu_back(hidden_grad)[0].astype(jnp.bfloat16)
    fc1_bias_grad = jnp.sum(pre_grad, axis=0, dtype=jnp.float32)
    fc1_grad_group = lax.dot_general(
        inputs_two, pre_grad, contract_rows, preferred_element_type=jnp.float32
    )
    row_block = pre_grad
    normed_two_grad = lax.psum_scatter(
        lax.dot_general(row_block, full_fc1, contract_cols, preferred_element_type=jnp.float32),
        "tensor",
        scatter_dimension=0,
        tiled=True,
    )
    norm_two_value, norm_two_back = jax.vjp(normalize, resid, ln2_gain, ln2_bias)
    resid_back, gain_two_grad, bias_two_grad = norm_two_back(normed_two_grad)
    resid_grad = cot_float + resid_back
    out_bias_grad = jnp.sum(resid_grad, axis=0)
    fc2_bias_grad = jnp.sum(cot_float, axis=0)
    resid_low = resid_grad.astype(jnp.bfloat16)
    resid_group = lax.all_gather(resid_low, "tensor", axis=0, tiled=True)
    out_grad_group = lax.dot_general(
        head_mixed, resid_group, contract_rows, preferred_element_type=jnp.float32
    )
    mixed_grad = lax.dot_general(
        resid_group, full_out, contract_cols, preferred_element_type=jnp.float32
    ).astype(jnp.bfloat16)
    query_grad, key_grad, value_grad = lax.map(
        attend_back, (query_heads, key_heads, value_heads, mixed_grad.reshape(head_shape), row_lse)
    )
    stacked_grads = jnp.stack(
        [
            query_grad.reshape(group_rows, local_width),
            key_grad.reshape(group_rows, local_width),
            value_grad.reshape(group_rows, local_width),
        ]
    )
    qkv_grad_group = jnp.einsum(
        "td,cte->cde", inputs_one, stacked_grads, preferred_element_type=jnp.float32
    )
    qv_bias_grad = jnp.stack(
        [
            jnp.sum(stacked_grads[0], axis=0, dtype=jnp.float32),
            jnp.sum(stacked_grads[2], axis=0, dtype=jnp.float32),
        ]
    )
    row_block = stacked_grads
    normed_one_grad = lax.psum_scatter(
        jnp.einsum("cte,cde->td", row_block, full_qkv, preferred_element_type=jnp.float32),
        "tensor",
        scatter_dimension=0,
        tiled=True,
    )
    norm_one_value, norm_one_back = jax.vjp(normalize, input_float, ln1_gain, ln1_bias)
    input_back, gain_one_grad, bias_one_grad = norm_one_back(normed_one_grad)
    input_grad = (resid_grad + input_back).astype(jnp.bfloat16)
    grad_w_qkv, grad_w_out, grad_w_fc1, grad_w_fc2 = (
        lax.psum_scatter(qkv_grad_group, "dp", scatter_dimension=1, tiled=True),
        lax.psum_scatter(out_grad_group, "dp", scatter_dimension=1, tiled=True),
        lax.psum_scatter(fc1_grad_group, "dp", scatter_dimension=0, tiled=True),
        lax.psum_scatter(fc2_grad_group, "dp", scatter_dimension=1, tiled=True),
    )
    vector_sums = lax.psum(
        (gain_one_grad, bias_one_grad, gain_two_grad, bias_two_grad, out_bias_grad, fc2_bias_grad),
        ("dp", "tensor"),
    )
    qv_sum, fc1_sum = lax.psum((qv_bias_grad, fc1_bias_grad), "dp")
    return (
        layer_output,
        input_grad,
        grad_w_qkv,
        qv_sum,
        grad_w_out,
        vector_sums[4],
        grad_w_fc1,
        fc1_sum,
        grad_w_fc2,
        vector_sums[5],
        vector_sums[0],
        vector_sums[1],
        vector_sums[2],
        vector_sums[3],
    )


def solution(mesh):
    return jax.shard_map(
        local,
        mesh=mesh,
        in_specs=(
            P(("dp", "tensor"), None),
            P("dp"),
            P(None, "dp", "tensor"),
            P(None, "tensor"),
            P("tensor", "dp"),
            P(),
            P("dp", "tensor"),
            P("tensor"),
            P("tensor", "dp"),
            P(),
            P(),
            P(),
            P(),
            P(),
            P(("dp", "tensor"), None),
        ),
        out_specs=(
            P(("dp", "tensor"), None),
            P(("dp", "tensor"), None),
            P(None, "dp", "tensor"),
            P(None, "tensor"),
            P("tensor", "dp"),
            P(),
            P("dp", "tensor"),
            P("tensor"),
            P("tensor", "dp"),
            P(),
            P(),
            P(),
            P(),
            P(),
        ),
        check_vma=False,
    )
```

profile of v0, /device:TPU:0, one launch (start us, length us, event | category | flops | bytes accessed | tf_op | source)
XLA Modules:
  0.0 1221.7 jit_solution(3025448042914870708)
XLA Ops:
  15.8 37.6 %all-gather.9.cloned.1.call-done = bf16[1168,1024]{1,0:T(8,128)(2,1)} async-done(((bf16[584,1024]{1,0:T(8,128)(2,1)}), bf16[1168,1024]{1,0:T(8,128)(2,1)}) %all-gather.9.cloned.1.call-update) | async-done | bytes 2392080 | tf_op jit(solution)/shard_map/all_gather | solution.py:115
  53.4 47.4 %all-gather.11.cloned.1.call-done = bf16[3,1024,512]{2,1,0:T(8,128)(2,1)} async-done(((bf16[3,64,512]{2,1,0:T(8,128)(2,1)}), bf16[3,1024,512]{2,1,0:T(8,128)(2,1)}) %all-gather.11.cloned.1.call-update) | async-done | bytes 3145744 | tf_op jit(solution)/shard_map/all_gather | solution.py:108
  100.8 6.5 convolution_bitcast_fusion
  112.6 3.6 squeeze.33
  127.4 4.7 squeeze.32
  137.5 20.1 %while.26 = (s32[]{:T(128)}, bf16[2,584,8,64]{1,3,2,0:T(8,128)(2,1)}, f32[2,8,584]{2,1,0:T(8,128)S(1)}, bf16[2,584,8,64]{1,3,2,0:T(8,128)(2,1)}, bf16[2,584,8,64...) while((s32[]{:T(128)}, bf16[2,584,8,64]{1,3,2,0:T(8,128)(2,1)}, ...), condition=%wide.region_5.6_spmd, body=%wide.region_2.5_spmd.sunk | while | flops 731518976 | bytes 50925628 | solution.py:125
  153.0 3.4 fusion.146
  157.5 4.7 copy.99
  162.3 4.2 reshape.184
  166.5 5.4 fusion.98
  172.6 59.1 %reduce-scatter.8.cloned.1.call-done = f32[584,1024]{1,0:T(8,128)} async-done(((f32[1168,1024]{1,0:T(8,128)}), f32[584,1024]{1,0:T(8,128)}) %reduce-scatter.8.cloned.1.call-update) | async-done | bytes 2392080 | tf_op jit(solution)/shard_map/reduce_scatter | solution.py:128
  240.7 43.8 %all-gather.17.cloned.1.call-done = bf16[1024,2048]{1,0:T(8,128)(2,1)} async-done(((bf16[64,2048]{1,0:T(8,128)(2,1)}), bf16[1024,2048]{1,0:T(8,128)(2,1)}) %all-gather.17.cloned.1.call-update) | async-done | bytes 4194320 | tf_op jit(solution)/shard_map/all_gather | solution.py:110
  284.5 36.9 %all-gather.15.cloned.1.call-done = bf16[1168,1024]{1,0:T(8,128)(2,1)} async-done(((bf16[584,1024]{1,0:T(8,128)(2,1)}), bf16[1168,1024]{1,0:T(8,128)(2,1)}) %all-gather.15.cloned.1.call-update) | async-done | bytes 2392080 | tf_op jit(solution)/shard_map/all_gather | solution.py:136
  321.5 10.0 convolution_add_fusion
  331.5 28.6 %all-gather.21.cloned.1.call-done = bf16[1168,1024]{1,0:T(8,128)(2,1)} async-done(((bf16[584,1024]{1,0:T(8,128)(2,1)}), bf16[1168,1024]{1,0:T(8,128)(2,1)}) %all-gather.21.cloned.1.call-update) | async-done | bytes 2392080 | tf_op jit(solution)/shard_map/all_gather | solution.py:149
  360.0 52.8 %all-gather.19.cloned.1.call-done = bf16[2048,1024]{0,1:T(8,128)(2,1)} async-done(((bf16[2048,64]{0,1:T(8,128)(2,1)}), bf16[2048,1024]{0,1:T(8,128)(2,1)}) %all-gather.19.cloned.1.call-update) | async-done | bytes 4194320 | tf_op jit(solution)/shard_map/all_gather | solution.py:111
  412.8 31.5 %convert_reduce_fusion = (f32[2048]{0:T(1024)}, bf16[1168,2048]{1,0:T(8,128)(2,1)S(1)}, f32[1168,2048]{1,0:T(8,128)}) fusion(f32[1168,2048]{1,0:T(8,128)} %convolution_add_fusion, bf16[1168,1024]{1,0:T(8,128)(2,1)} %all-gather.21.cloned.1.call-done, bf16[2048,1024]{0,1:T(8,128)(2,1)} %all-gather.19.cloned.1.call-done), kind=kOutput, calls=%fused_computation.66 | convolution fusion | flops 5075957760 | bytes 30515200 | tf_op jit(solution)/shard_map/dot_general | solution.py:153
  446.4 6.9 fusion.99
  453.8 12.0 multiply_convert_fusion.1
  465.8 9.7 convolution_convert_fusion
  475.7 37.0 %reduce-scatter.12.cloned.1.call-done = f32[584,1024]{1,0:T(8,128)} async-done(((f32[1168,1024]{1,0:T(8,128)}), f32[584,1024]{1,0:T(8,128)}) %reduce-scatter.12.cloned.1.call-update) | async-done | bytes 2392080 | tf_op jit(solution)/shard_map/reduce_scatter | solution.py:163
  515.8 34.1 %reduce-scatter.10.cloned.1.call-done = bf16[584,1024]{1,0:T(8,128)(2,1)} async-done(((bf16[1168,1024]{1,0:T(8,128)(2,1)}), bf16[584,1024]{1,0:T(8,128)(2,1)}) %reduce-scatter.10.cloned.1.call-update) | async-done | bytes 1196048 | tf_op jit(solution)/shard_map/reduce_scatter | solution.py:140
  549.9 4.1 fusion.93
  557.1 36.5 %all-gather.23.cloned.1.call-done = bf16[1168,1024]{1,0:T(8,128)(2,1)} async-done(((bf16[584,1024]{1,0:T(8,128)(2,1)}), bf16[1168,1024]{1,0:T(8,128)(2,1)}) %all-gather.23.cloned.1.call-update) | async-done | bytes 2392080 | tf_op jit(solution)/shard_map/all_gather | solution.py:175
  593.6 4.1 convolution_convert_fusion.1
  607.6 45.2 %while.27 = (s32[]{:T(128)}, bf16[2,584,8,64]{1,3,2,0:T(8,128)(2,1)}, bf16[2,584,8,64]{1,3,2,0:T(8,128)(2,1)}, bf16[2,584,8,64]{1,3,2,0:T(8,128)(2,1)}, bf16[2,5...) while((s32[]{:T(128)}, ...), condition=%wide.region_16.17_spmd, body=%wide.region_14.16_spmd.sunk | while | flops 1788624384 | bytes 129962736 | solution.py:182
  612.7 6.6 multiply_reduce_fusion.5
  619.2 6.7 multiply_convert_fusion.4
  635.2 6.6 multiply_reduce_fusion.5
  641.8 6.7 multiply_convert_fusion.4
  652.8 3.9 copy.119
  656.7 4.5 reshape.189
  664.0 3.5 reshape.191
  667.5 3.9 copy.120
  671.4 4.2 reshape.190
  680.3 6.3 convolution_bitcast_fusion.2
  686.5 9.4 copy.111
  696.0 9.1 convolution_bitcast_fusion.1
  705.1 10.6 fusion.101
  715.8 10.9 fusion.102
  726.8 5.1 fusion.100
  735.2 62.8 %all-reduce.2 = (f32[2,512]{1,0:T(2,128)}, f32[2048]{0:T(1024)}) all-reduce(f32[2,512]{1,0:T(2,128)S(1)} %pad_maximum_fusion, f32[2048]{0:T(1024)S(1)} %copy-done.55), channel_id=1, replica_groups=mesh['dp'=16,'tensor'=2] {'dp'}, use_global_device_ids=true, to_apply=%region_23.24 | all-reduce | flops 3072 | bytes 24576 | tf_op jit(solution)/shard_map/psum | solution.py:221
  798.0 68.6 %all-reduce.5.cloned.1.call-done = f32[3,1024,512]{2,0,1:T(4,128)} async-done(((f32[3,1024,512]{2,0,1:T(4,128)}), f32[3,1024,512]{2,0,1:T(4,128)}) %all-reduce.5.cloned.1.call-update) | async-done | bytes 6291472
  868.6 61.0 %reduce-scatter.14.cloned.1.call-done = f32[584,1024]{1,0:T(8,128)} async-done(((f32[1168,1024]{1,0:T(8,128)}), f32[584,1024]{1,0:T(8,128)}) %reduce-scatter.14.cloned.1.call-update) | async-done | bytes 2392080 | tf_op jit(solution)/shard_map/reduce_scatter | solution.py:202
  936.5 40.2 %all-reduce.1 = (f32[1024]{0:T(1024)}, f32[1024]{0:T(1024)}, f32[1024]{0:T(1024)}, f32[1024]{0:T(1024)}, f32[1024]{0:T(1024)}, /*index=5*/f32[1024]{0:T(1024)}) all-reduce(f32[1024]{0:T(1024)S(1)} %get-tuple-element.225, f32[1024]{0:T(1024)S(1)} %get-tuple-element.224, ...), channel_id=1, replica_groups=mesh['dp'=16,'tensor'=2] {'dp','tensor'}, use_global_device_ids=true, to_apply=%region_26.27 | all-reduce | flops 6144 | bytes 49152 | tf_op jit(solution)/shard_map/psum | solution.py:217
  976.7 62.6 %reduce-scatter.18.cloned.1.call-done = f32[64,2048]{1,0:T(8,128)} async-done(((f32[1024,2048]{1,0:T(8,128)}), f32[64,2048]{1,0:T(8,128)}) %reduce-scatter.18.cloned.1.call-update) | async-done | bytes 524304 | tf_op jit(solution)/shard_map/reduce_scatter | solution.py:214
  1039.2 109.4 %reduce-scatter.20.cloned.1.call-done = f32[2048,64]{0,1:T(8,128)} async-done(((f32[2048,1024]{0,1:T(8,128)}), f32[2048,64]{0,1:T(8,128)}) %reduce-scatter.20.cloned.1.call-update) | async-done | bytes 524304 | tf_op jit(solution)/shard_map/reduce_scatter | solution.py:215
  1148.7 66.0 %reduce-scatter.16.cloned.1.call-done = f32[512,64]{0,1:T(8,128)} async-done(((f32[512,1024]{0,1:T(8,128)}), f32[512,64]{0,1:T(8,128)}) %reduce-scatter.16.cloned.1.call-update) | async-done | bytes 131088 | tf_op jit(solution)/shard_map/reduce_scatter | solution.py:213
  (265 shorter events, 112.1 us)
Async XLA Ops:
  7.2 4.6 copy-start.6
  7.2 46.2 %all-gather.9.cloned.1.call-start = ((), (), s32[]{:S(2)}) async-start(), calls=%async_computation.7 | async-start | bytes 3588096 | tf_op jit(solution)/shard_map/all_gather | solution.py:115
  8.8 6.8 copy-start.58
  14.1 86.7 %all-gather.11.cloned.1.call-start = ((), (), s32[]{:S(2)}) async-start(), calls=%async_computation.8 | async-start | bytes 3342336 | tf_op jit(solution)/shard_map/all_gather | solution.py:108
  14.8 151.7 %all-gather.13.cloned.1.call-start = ((), (), s32[]{:S(2)}) async-start(), calls=%async_computation.9 | async-start | bytes 1114112 | tf_op jit(solution)/shard_map/all_gather | solution.py:109
  15.6 216.2 %reduce-scatter.8.cloned.1.call-start = ((), (), s32[]{:S(2)}) async-start(), calls=%async_computation.10 | async-start | bytes 7176192 | tf_op jit(solution)/shard_map/reduce_scatter | solution.py:128
  157.5 8.9 copy-start
  157.5 9.0 copy-start.2
  157.5 9.0 copy-start.30
  171.9 59.8 %copy-start.7 = (bf16[584,1024]{1,0:T(8,128)(2,1)S(1)}, bf16[584,1024]{1,0:T(8,128)(2,1)}, u32[]{:S(2)}) copy-start(bf16[584,1024]{1,0:T(8,128)(2,1)} %param.19) | copy-start | bytes 3588100
  171.9 59.8 %copy-start.59 = (f32[1024]{0:T(1024)S(1)}, f32[1024]{0:T(1024)}, u32[]{:S(2)}) copy-start(f32[1024]{0:T(1024)} %param.24) | copy-start | bytes 12292
  172.0 112.6 %all-gather.17.cloned.1.call-start = ((), (), s32[]{:S(2)}) async-start(), calls=%async_computation.12 | async-start | bytes 4456448 | tf_op jit(solution)/shard_map/all_gather | solution.py:110
  172.5 63.3 %copy-start.41 = (f32[1024]{0:T(1024)S(1)}, f32[1024]{0:T(1024)}, u32[]{:S(2)}) copy-start(f32[1024]{0:T(1024)} %param.31) | copy-start | bytes 12292
  172.6 63.3 %copy-start.57 = (f32[1024]{0:T(1024)S(1)}, f32[1024]{0:T(1024)}, u32[]{:S(2)}) copy-start(f32[1024]{0:T(1024)} %param.32) | copy-start | bytes 12292
  172.6 148.9 %all-gather.15.cloned.1.call-start = ((), (), s32[]{:S(2)}) async-start(), calls=%async_computation.11 | async-start | bytes 3588096 | tf_op jit(solution)/shard_map/all_gather | solution.py:136
  237.3 84.1 %copy-start.63 = (f32[2048]{0:T(1024)S(1)}, f32[2048]{0:T(1024)}, u32[]{:S(2)}) copy-start(f32[2048]{0:T(1024)} %param.26) | copy-start | bytes 24580
  237.4 122.7 %all-gather.21.cloned.1.call-start = ((), (), s32[]{:S(2)}) async-start(), calls=%async_computation.15 | async-start | bytes 3588096 | tf_op jit(solution)/shard_map/all_gather | solution.py:149
  239.9 172.9 %all-gather.19.cloned.1.call-start = ((), (), s32[]{:S(2)}) async-start(), calls=%async_computation.13 | async-start | bytes 4456448 | tf_op jit(solution)/shard_map/all_gather | solution.py:111
  240.7 272.0 %reduce-scatter.12.cloned.1.call-start = ((), (), s32[]{:S(2)}) async-start(), calls=%async_computation.16 | async-start | bytes 7176192 | tf_op jit(solution)/shard_map/reduce_scatter | solution.py:163
  412.8 33.6 %copy-start.60 = (bf16[1024,2048]{1,0:T(8,128)(2,1)S(1)}, bf16[1024,2048]{1,0:T(8,128)(2,1)}, u32[]{:S(2)}) copy-start(bf16[1024,2048]{1,0:T(8,128)(2,1)} %all-gather.17.cloned.1.call-done) | copy-start | bytes 12582916
  453.4 96.6 %reduce-scatter.10.cloned.1.call-start = ((), (), s32[]{:S(2)}) async-start(), calls=%async_computation.14 | async-start | bytes 3588096 | tf_op jit(solution)/shard_map/reduce_scatter | solution.py:140
  465.8 46.9 %copy-start.35 = (f32[584]{0:T(1024)S(1)}, f32[584]{0:T(1024)}, u32[]{:S(2)}) copy-start(f32[584]{0:T(1024)} %copy-done.34) | copy-start | bytes 7012
  465.8 46.9 %copy-start.37 = (f32[584]{0:T(1024)S(1)}, f32[584]{0:T(1024)}, u32[]{:S(2)}) copy-start(f32[584]{0:T(1024)} %copy-done.36) | copy-start | bytes 7012
  465.8 46.9 %copy-start.42 = (f32[1024]{0:T(1024)S(1)}, f32[1024]{0:T(1024)}, u32[]{:S(2)}) copy-start(f32[1024]{0:T(1024)} %param.31) | copy-start | bytes 12292
  475.5 37.2 %copy-start.5 = (f32[584,1024]{1,0:T(8,128)S(1)}, f32[584,1024]{1,0:T(8,128)}, u32[]{:S(2)}) copy-start(f32[584,1024]{1,0:T(8,128)} %copy-done.4) | copy-start | bytes 7176196
  475.6 40.2 %copy-start.48 = (f32[584]{0:T(1024)S(1)}, f32[584]{0:T(1024)}, u32[]{:S(2)}) copy-start(f32[584]{0:T(1024)} %copy-done.47) | copy-start | bytes 7012
  475.6 74.3 %copy-start.52 = (f32[584]{0:T(1024)S(1)}, f32[584]{0:T(1024)}, u32[]{:S(2)}) copy-start(f32[584]{0:T(1024)} %get-tuple-element.272) | copy-start | bytes 7012
  475.6 74.3 %copy-start.56 = (f32[1024]{0:T(1024)S(1)}, f32[1024]{0:T(1024)}, u32[]{:S(2)}) copy-start(f32[1024]{0:T(1024)} %param.28) | copy-start | bytes 12292
  475.6 118.0 %all-gather.23.cloned.1.call-start = ((), (), s32[]{:S(2)}) async-start(), calls=%async_computation.17 | async-start | bytes 3588096 | tf_op jit(solution)/shard_map/all_gather | solution.py:175
  549.9 5.6 copy-start.21
  549.9 5.6 copy-start.50
  555.5 38.1 %copy-start.62 = (bf16[512,1024]{0,1:T(8,128)(2,1)S(1)}, bf16[512,1024]{0,1:T(8,128)(2,1)}, u32[]{:S(2)}) copy-start(bf16[512,1024]{0,1:T(8,128)(2,1)} %all-gather.13.cloned.1.call-done) | copy-start | bytes 3145732
  557.0 309.6 %all-reduce.5.cloned.1.call-start = ((), (), s32[]{:S(2)}) async-start(), calls=%async_computation.22 | async-start | bytes 16777216
  612.7 6.6 copy-start.16
  619.2 6.8 copy-start.23
  635.2 6.6 copy-start.16
  641.8 6.8 copy-start.23
  656.7 4.5 copy-start.17
  696.0 233.6 %reduce-scatter.14.cloned.1.call-start = ((), (), s32[]{:S(2)}) async-start(), calls=%async_computation.18 | async-start | bytes 7176192 | tf_op jit(solution)/shard_map/reduce_scatter | solution.py:202
  705.1 334.2 %reduce-scatter.18.cloned.1.call-start = ((), (), s32[]{:S(2)}) async-start(), calls=%async_computation.20 | async-start | bytes 8912896 | tf_op jit(solution)/shard_map/reduce_scatter | solution.py:214
  715.8 432.9 %reduce-scatter.20.cloned.1.call-start = ((), (), s32[]{:S(2)}) async-start(), calls=%async_computation.21 | async-start | bytes 8912896 | tf_op jit(solution)/shard_map/reduce_scatter | solution.py:215
  726.7 5.2 copy-start.65
  726.7 488.0 %reduce-scatter.16.cloned.1.call-start = ((), (), s32[]{:S(2)}) async-start(), calls=%async_computation.19 | async-start | bytes 2228224 | tf_op jit(solution)/shard_map/reduce_scatter | solution.py:213
  731.9 197.7 %copy-start.8 = (bf16[584,1024]{1,0:T(8,128)(2,1)S(1)}, bf16[584,1024]{1,0:T(8,128)(2,1)}, u32[]{:S(2)}) copy-start(bf16[584,1024]{1,0:T(8,128)(2,1)} %param.19) | copy-start | bytes 3588100
  731.9 197.7 %copy-start.33 = (f32[584]{0:T(1024)S(1)}, f32[584]{0:T(1024)}, u32[]{:S(2)}) copy-start(f32[584]{0:T(1024)} %copy-done.32) | copy-start | bytes 7012
  731.9 197.7 %copy-start.38 = (f32[1024]{0:T(1024)S(1)}, f32[1024]{0:T(1024)}, u32[]{:S(2)}) copy-start(f32[1024]{0:T(1024)} %param.29) | copy-start | bytes 12292
  798.0 134.1 %copy-start.46 = (f32[584]{0:T(1024)S(1)}, f32[584]{0:T(1024)}, u32[]{:S(2)}) copy-start(f32[584]{0:T(1024)} %copy-done.45) | copy-start | bytes 7012
  798.0 134.1 %copy-start.40 = (f32[584]{0:T(1024)S(1)}, f32[584]{0:T(1024)}, u32[]{:S(2)}) copy-start(f32[584]{0:T(1024)} %copy-done.39) | copy-start | bytes 7012
  (46 other events, 91.4 us)
Sparse Core Ops, SparseCore 0:
  14.2 39.1 all-gather.8
  55.6 45.2 all-gather.10
  103.0 36.7 all-gather.12
  172.1 59.6 reduce-scatter.7
  233.8 50.7 all-gather.16
  286.5 34.9 all-gather.14
  323.6 36.4 all-gather.20
  362.2 50.5 all-gather.18
  453.5 59.1 reduce-scatter.11
  514.8 35.0 reduce-scatter.9
  557.1 36.4 all-gather.22
  696.1 170.4 all-reduce.4
  869.0 60.5 reduce-scatter.13
  934.6 104.5 reduce-scatter.17
  1044.3 104.3 reduce-scatter.19
  1153.3 61.3 reduce-scatter.15
where the time goes:
time: 1230 us; the launch traced here: 1220 us
  waiting for transfers between devices  784 us (64%)
  matrix products  158 us (13%)
  blocking collectives  103 us (8%)
  local copies, waits for them, and re-layouts  97 us (8%)
  other arithmetic  62.4 us (5%)
  between operations  15.5 us (1%)
    reduce_scatter x1, waiting for transfers between devices, local(): lax.psum_scatter(fc2_grad_group, 'dp', scatter_dimension=1, tiled=True)  109 us
    unnamed x17, waiting for transfers between devices  71.4 us
    reduce_scatter x1, waiting for transfers between devices, local(): lax.psum_scatter(out_grad_group, 'dp', scatter_dimension=1, tiled=True)  66 us
    psum x1, blocking collectives, local(): qv_sum, fc1_sum = lax.psum((qv_bias_grad, fc1_bias_grad), 'dp')  62.8 us
    reduce_scatter x1, waiting for transfers between devices, local(): lax.psum_scatter(fc1_grad_group, 'dp', scatter_dimension=0, tiled=True)  62.6 us
    reduce_scatter x1, waiting for transfers between devices, local(): lax.psum_scatter(jnp.einsum('cte,cde->td', row_block, full_qkv, preferred...  61 us
    reduce_scatter x1, waiting for transfers between devices, local(): lax.psum_scatter(jnp.dot(row_block, full_out, preferred_element_type=jnp....  59.1 us
    all_gather x1, waiting for transfers between devices, local(): lax.all_gather(w_fc2, 'dp', axis=1, tiled=True)  52.8 us
  transfers between devices with their start and end apart: 16, of which 15 were waited for; matrix products, arithmetic and copies ran while one was open for 12% of the time, Pallas kernels for 0%

commit v1 on v0

--- a/solution.py
+++ b/solution.py
@@ -1,6 +1,10 @@
+import functools
+
 import jax
 import jax.numpy as jnp
 from jax import lax
+from jax.experimental import pallas as pl
+from jax.experimental.pallas import tpu as pltpu
 from jax.sharding import PartitionSpec as P
 
 HEADS = 16
@@ -72,7 +76,7 @@
     )
 
 
-def local(
+def split_heads(
     block_input,
     image_mask,
     w_qkv,
@@ -237,9 +241,318 @@
     )
 
 
+BIT_X, BIT_CORE, BIT_Y, BIT_Z_LOW, BIT_Z_HIGH = 1, 2, 4, 8, 16
+AXES = ("dp", "tensor")
+
+
+def exchange(block, bit):
+    return lax.ppermute(block, AXES, [(src, src ^ bit) for src in range(32)])
+
+
+def gather_weights(shard):
+    half = shard.shape[1] // 2
+    block = jnp.concatenate([shard, exchange(shard, BIT_Z_HIGH)], axis=0)
+    first = exchange(block[:, :half], BIT_X)
+    second = exchange(block[:, half:], BIT_Y)
+    block = jnp.stack([block, jnp.concatenate([first, second], axis=1)])
+    block = jnp.concatenate([block, exchange(block, BIT_Z_LOW)], axis=1)
+    first = exchange(block[:, :, :half], BIT_Y)
+    second = exchange(block[:, :, half:], BIT_X)
+    near = (block, first, second)
+    far = tuple(exchange(piece, BIT_CORE) for piece in near)
+    return near, far
+
+
+def assemble(pieces):
+    sides = []
+    for side in range(2):
+        columns = []
+        low, high = [], []
+        for block, first, second in pieces:
+            half = first.shape[2]
+            low += [block[side, :, :half], first[side]]
+            high += [block[0, :, half:], block[1, :, half:]] if side == 0 else [second[0], second[1]]
+        sides.append(jnp.concatenate([jnp.concatenate(low, axis=0), jnp.concatenate(high, axis=0)], axis=1))
+    return sides
+
+
+def scatter_grads(sides):
+    grads = jnp.stack(sides)
+    half = grads.shape[2] // 2
+    low = jnp.bfloat16
+    block = (grads[:, :512] + exchange(grads[:, 512:], BIT_CORE)).astype(low)
+    first = block[:, :256, :half] + exchange(block[:, 256:, :half], BIT_Y)
+    second = block[0, :, half:] + exchange(block[1, :, half:], BIT_X)
+    block = jnp.concatenate([first, second.reshape(2, 256, half)], axis=2)
+    block = block[:, :128] + exchange(block[:, 128:], BIT_Z_LOW)
+    first = block[0, :, :half] + exchange(block[1, :, :half], BIT_X)
+    second = block[0, :, half:] + exchange(block[1, :, half:], BIT_Y)
+    block = jnp.concatenate([first, second], axis=1)
+    other = exchange(block[64:], BIT_Z_HIGH)
+    return block[:64].astype(jnp.float32) + other.astype(jnp.float32)
+
+
+def total(vectors, bits):
+    for bit in bits:
+        vectors = vectors + exchange(vectors, bit)
+    return vectors
+
+
+def place_matrix():
+    relative = lax.broadcasted_iota(jnp.int32, (1024, 1024), 1)
+    feature = lax.broadcasted_iota(jnp.int32, (1024, 1024), 0)
+    block = relative // 64
+    shard = (block // 8) + 2 * (block // 4 % 2) + 4 * (block // 2 % 2) + 8 * (block % 2)
+    shard = shard ^ lax.axis_index("dp")
+    return (feature == shard * 64 + relative % 64).astype(jnp.bfloat16)
+
+
+def attend_kernel(q_ref, k_ref, v_ref, o_ref, lse_ref):
+    queries, keys, values = q_ref[...], k_ref[...], v_ref[...]
+    queries = queries * jnp.bfloat16(0.125)
+    lane = lax.broadcasted_iota(jnp.int32, keys.shape, 1)
+    mixed = []
+    for head in range(2):
+        own = (lane // 64) == head
+        scores = lax.dot_general(
+            jnp.where(own, keys, 0), queries, (((1,), (1,)), ((), ())), preferred_element_type=jnp.float32
+        )
+        valid = lax.broadcasted_iota(jnp.int32, scores.shape, 0) < VALID
+        scores = jnp.where(valid, scores, masked_score)
+        top = jnp.max(scores, axis=0, keepdims=True)
+        expo = jnp.exp(scores - top)
+        norm = jnp.sum(expo, axis=0, keepdims=True)
+        out = lax.dot_general(
+            values, expo.astype(jnp.bfloat16), (((0,), (0,)), ((), ())), preferred_element_type=jnp.float32
+        )
+        mixed.append(out[head * 64 : head * 64 + 64] / norm)
+        lse_ref[0, head : head + 1, :] = top + jnp.log(norm)
+    o_ref[...] = jnp.concatenate(mixed, axis=0).T.astype(jnp.bfloat16)
+
+
+def attend(projected):
+    rows = projected.shape[0]
+    images = rows // SEQ
+
+    def column(offset):
+        return lambda image, pair: (image, (pair // 4) * 12 + offset + pair % 4)
+
+    return pl.pallas_call(
+        attend_kernel,
+        grid=(images, 8),
+        in_specs=[pl.BlockSpec((SEQ, 128), column(4 * c)) for c in range(3)],
+        out_specs=[
+            pl.BlockSpec((SEQ, 128), lambda image, pair: (image, pair)),
+            pl.BlockSpec((1, 2, SEQ), lambda image, pair: (image * 8 + pair, 0, 0)),
+        ],
+        out_shape=[
+            jax.ShapeDtypeStruct((rows, 1024), jnp.bfloat16),
+            jax.ShapeDtypeStruct((images * 8, 2, SEQ), jnp.float32),
+        ],
+        compiler_params=pltpu.CompilerParams(vmem_limit_bytes=24 << 20),
+        cost_estimate=pl.CostEstimate(flops=images * 14 * 10**9, bytes_accessed=images * 5 * 10**6, transcendentals=images * 6 * 10**6),
+    )(projected, projected, projected)
+
+
+def attend_back_kernel(q_ref, k_ref, v_ref, do_ref, lse_ref, dq_ref, dk_ref, dv_ref):
+    queries, keys, values, mixed_grad = q_ref[...], k_ref[...], v_ref[...], do_ref[...]
+    queries = queries * jnp.bfloat16(0.125)
+    lane = lax.broadcasted_iota(jnp.int32, keys.shape, 1)
+    dq, dk, dv = [], [], []
+    for head in range(2):
+        own = (lane // 64) == head
+        scores = lax.dot_general(
+            jnp.where(own, keys, 0), queries, (((1,), (1,)), ((), ())), preferred_element_type=jnp.float32
+        )
+        valid = lax.broadcasted_iota(jnp.int32, scores.shape, 0) < VALID
+        probs = jnp.where(valid, jnp.exp(scores - lse_ref[0, head : head + 1, :]), 0)
+        dv.append(jnp.dot(probs.astype(jnp.bfloat16), mixed_grad, preferred_element_type=jnp.float32))
+        back = lax.dot_general(
+            jnp.where(own, values, 0), mixed_grad, (((1,), (1,)), ((), ())), preferred_element_type=jnp.float32
+        )
+        row = jnp.sum(probs * back, axis=0, keepdims=True)
+        score_grad = (probs * (back - row)).astype(jnp.bfloat16)
+        dk.append(jnp.dot(score_grad, queries, preferred_element_type=jnp.float32))
+        out = lax.dot_general(
+            keys, score_grad, (((0,), (0,)), ((), ())), preferred_element_type=jnp.float32
+        )
+        dq.append(out[head * 64 : head * 64 + 64] * 0.125)
+    low = lane < 64
+    dq_ref[...] = jnp.concatenate(dq, axis=0).T.astype(jnp.bfloat16)
+    dk_ref[...] = jnp.where(low, dk[0], dk[1]).astype(jnp.bfloat16)
+    dv_ref[...] = jnp.where(low, dv[0], dv[1]).astype(jnp.bfloat16)
+
+
+def attend_back_all(projected, mixed_grad, lse):
+    rows = projected.shape[0]
+    images = rows // SEQ
+
+    def column(offset):
+        return lambda image, pair: (image, (pair // 4) * 12 + offset + pair % 4)
+
+    return pl.pallas_call(
+        attend_back_kernel,
+        grid=(images, 8),
+        in_specs=[pl.BlockSpec((SEQ, 128), column(4 * c)) for c in range(3)]
+        + [
+            pl.BlockSpec((SEQ, 128), lambda image, pair: (image, pair)),
+            pl.BlockSpec((1, 2, SEQ), lambda image, pair: (image * 8 + pair, 0, 0)),
+        ],
+        out_specs=[pl.BlockSpec((SEQ, 128), lambda image, pair: (image, pair))] * 3,
+        out_shape=[jax.ShapeDtypeStruct((rows, 1024), jnp.bfloat16)] * 3,
+        compiler_params=pltpu.CompilerParams(vmem_limit_bytes=32 << 20),
+        cost_estimate=pl.CostEstimate(flops=images * 28 * 10**9, bytes_accessed=images * 9 * 10**6, transcendentals=images * 6 * 10**6),
+    )(projected, projected, projected, mixed_grad, lse)
+
+
+def own_images(
+    block_input,
+    image_mask,
+    w_qkv,
+    b_qv,
+    w_out,
+    b_out,
+    w_fc1,
+    b_fc1,
+    w_fc2,
+    b_fc2,
+    ln1_gain,
+    ln1_bias,
+    ln2_gain,
+    ln2_bias,
+    grad_out,
+):
+    f32, low = jnp.float32, jnp.bfloat16
+    rows = block_input.shape[0]
+    tensor_index = lax.axis_index("tensor")
+    token_index = tensor_index * rows + jnp.arange(rows)
+    image_pick = ((token_index // SEQ)[:, None] == jnp.arange(image_mask.shape[0])[None, :]).astype(f32)
+    token_keep = jnp.sum(image_pick * image_mask.astype(f32)[None, :], axis=1)
+    token_keep = token_keep * (token_index % SEQ < VALID).astype(f32)
+
+    def rows_of(left, right):
+        return lax.dot_general(left, right, (((0,), (0,)), ((), ())), preferred_element_type=f32)
+
+    def cols_of(left, right):
+        return lax.dot_general(left, right, (((1,), (1,)), ((), ())), preferred_element_type=f32)
+
+    def dot(left, right):
+        return jnp.dot(left, right, preferred_element_type=f32)
+
+    attn_shard = jnp.concatenate([w_qkv[0], w_qkv[1], w_qkv[2], w_out.T], axis=1)
+    attn_pieces = gather_weights(attn_shard)
+    fc1_pieces = gather_weights(w_fc1)
+    fc2_pieces = gather_weights(w_fc2.T)
+    bias_own = jnp.concatenate([b_qv.reshape(-1), b_fc1])[None, :]
+    bias_sides = jnp.concatenate([bias_own, exchange(bias_own, BIT_X)], axis=0)
+
+    place = place_matrix()
+    vectors = jnp.stack([b_out, b_fc2, ln1_gain, ln1_bias, ln2_gain, ln2_bias])
+    vectors = jnp.dot(vectors, place.astype(f32), precision=lax.Precision.HIGHEST)
+    b_out, b_fc2, ln1_gain, ln1_bias, ln2_gain, ln2_bias = vectors
+    signal = dot(block_input, place)
+    cot_low = dot(grad_out * token_keep.astype(low)[:, None], place).astype(low)
+    cot = cot_low.astype(f32)
+
+    normed_one = normalize(signal, ln1_gain, ln1_bias).astype(low)
+    w_attn = assemble(attn_pieces)
+    projected = []
+    for side in range(2):
+        bias = bias_sides[side]
+        bias = jnp.concatenate([bias[:512], jnp.zeros((512,), f32), bias[512:1024]])
+        projected.append((dot(normed_one, w_attn[side][:, :1536]) + bias).astype(low))
+    projected = jnp.concatenate(projected, axis=1)
+    mixed, lse = attend(projected)
+    attn = sum(cols_of(mixed[:, side * 512 : side * 512 + 512], w_attn[side][:, 1536:]) for side in range(2))
+    resid = signal + (attn + b_out)
+    normed_two = normalize(resid, ln2_gain, ln2_bias).astype(low)
+    w_one = assemble(fc1_pieces)
+    hidden, slope = [], []
+    for side in range(2):
+        pre = dot(normed_two, w_one[side]) + bias_sides[side, 1024:]
+        phi = 0.5 * (1.0 + lax.erf(pre * (0.5**0.5)))
+        hidden.append((pre * phi).astype(low))
+        slope.append((phi + pre * (jnp.exp(-0.5 * pre * pre) * (0.5 / 3.141592653589793) ** 0.5)).astype(low))
+    fc2_grad = scatter_grads([rows_of(cot_low, hidden[side]).astype(low) for side in range(2)])
+    w_two = assemble(fc2_pieces)
+    pre_grad = [(dot(cot_low, w_two[side]) * slope[side].astype(f32)).astype(low) for side in range(2)]
+    fc1_grad = scatter_grads([rows_of(normed_two, pre_grad[side]).astype(low) for side in range(2)])
+    fc1_bias_grad = jnp.stack([jnp.sum(pre_grad[side], axis=0, dtype=f32) for side in range(2)])
+    normed_two_grad = sum(cols_of(pre_grad[side], w_one[side]) for side in range(2))
+    _, norm_two_back = jax.vjp(normalize, resid, ln2_gain, ln2_bias)
+    resid_back, gain_two_grad, bias_two_grad = norm_two_back(normed_two_grad)
+    resid_grad = cot + resid_back
+    resid_low = resid_grad.astype(low)
+    mixed_grad = jnp.concatenate([dot(resid_low, w_attn[side][:, 1536:]).astype(low) for side in range(2)], axis=1)
+    query_grad, key_grad, value_grad = attend_back_all(projected, mixed_grad, lse)
+    attn_grads, normed_one_grad = [], 0.0
+    for side in range(2):
+        part = slice(side * 512, side * 512 + 512)
+        side_grads = jnp.concatenate([query_grad[:, part], key_grad[:, part], value_grad[:, part]], axis=1)
+        attn_grads.append(
+            jnp.concatenate([rows_of(normed_one, side_grads), rows_of(resid_low, mixed[:, part])], axis=1).astype(low)
+        )
+        normed_one_grad = normed_one_grad + cols_of(side_grads, w_attn[side][:, :1536])
+    attn_grad = scatter_grads(attn_grads)
+    _, norm_one_back = jax.vjp(normalize, signal, ln1_gain, ln1_bias)
+    input_back, gain_one_grad, bias_one_grad = norm_one_back(normed_one_grad)
+    input_grad = cols_of((resid_grad + input_back).astype(low), place).astype(low)
+
+    mlp = sum(cols_of(hidden[side], w_two[side]) for side in range(2))
+    layer_output = ((resid + (mlp + b_fc2)) * token_keep[:, None]).astype(low)
+    layer_output = cols_of(layer_output, place).astype(low)
+
+    sums = jnp.stack(
+        [
+            gain_one_grad,
+            bias_one_grad,
+            gain_two_grad,
+            bias_two_grad,
+            jnp.sum(resid_grad, axis=0),
+            jnp.sum(cot, axis=0),
+        ]
+    )
+    sums = lax.dot_general(
+        sums, place.astype(f32), (((1,), (1,)), ((), ())), precision=lax.Precision.HIGHEST
+    )
+    sums = total(sums, (BIT_X, BIT_CORE, BIT_Y, BIT_Z_LOW, BIT_Z_HIGH))
+    side_sums = jnp.concatenate(
+        [
+            jnp.sum(query_grad, axis=0, dtype=f32).reshape(2, 512),
+            jnp.sum(value_grad, axis=0, dtype=f32).reshape(2, 512),
+            fc1_bias_grad,
+        ],
+        axis=1,
+    )
+    side_sums = side_sums[:1] + exchange(side_sums[1:], BIT_X)
+    side_sums = total(side_sums, (BIT_CORE, BIT_Y, BIT_Z_LOW, BIT_Z_HIGH))[0]
+    return (
+        layer_output,
+        input_grad,
+        attn_grad[:, :1536].reshape(64, 3, 512).transpose(1, 0, 2),
+        side_sums[:1024].reshape(2, 512),
+        attn_grad[:, 1536:].T,
+        sums[4],
+        fc1_grad,
+        side_sums[1024:],
+        fc2_grad.T,
+        sums[5],
+        sums[0],
+        sums[1],
+        sums[2],
+        sums[3],
+    )
+
+
 def solution(mesh):
+    def plan(block_input, *others):
+        whole_images = block_input.shape[0] % SEQ == 0
+        if whole_images and mesh.shape["dp"] == 16 and mesh.shape["tensor"] == 2:
+            return own_images(block_input, *others)
+        return split_heads(block_input, *others)
+
     return jax.shard_map(
-        local,
+        plan,
         mesh=mesh,
         in_specs=(
             P(("dp", "tensor"), None),

time: 1230 us -> 605 us (0.49)
  waiting for transfers between devices: 784 us -> 226 us
  blocking collectives: 103 us -> 0 us
  local copies, waits for them, and re-layouts: 97 us -> 37.9 us
  starting transfers between devices: 1.05 us -> 57.3 us
  Pallas kernels: 0 us -> 37.7 us
  between operations: 15.5 us -> 3.17 us
    reduce_scatter x7 -> x0, waiting for transfers between devices: 429 us -> none  [the longest x1 109 us: local(): lax.psum_scatter(fc2_grad_group, 'dp', scatter_dimension=1, tiled=True)]
    all_gather x8 -> x0, waiting for transfers between devices: 284 us -> none  [the longest x1 52.8 us: local(): lax.all_gather(w_fc2, 'dp', axis=1, tiled=True)]
    ppermute x0 -> x59, waiting for transfers between devices: none -> 226 us  [exchange(): return lax.ppermute(block, AXES, [(src, src ^ bit) for src in range(32)])]
    psum x2 -> x0, blocking collectives: 103 us -> none  [the longest x1 62.8 us: local(): qv_sum, fc1_sum = lax.psum((qv_bias_grad, fc1_bias_grad), 'dp')]
    unnamed x17 -> x0, waiting for transfers between devices: 71.4 us -> none
    ppermute x0 -> x59, starting transfers between devices: none -> 57.3 us  [exchange(): return lax.ppermute(block, AXES, [(src, src ^ bit) for src in range(32)])]
    pallas_call x0 -> x2, Pallas kernels: none -> 37.7 us  [the longest x1 23.2 us: attend_back_all(): pl.pallas_call(attend_back_kernel, grid=(images, 8), in_specs=[pl.BlockSp...]
    concatenate x0 -> x19, other arithmetic: none -> 33 us  [the longest x2 29.1 us: assemble(): jnp.concatenate([jnp.concatenate(low, axis=0), jnp.concatenate(high, axis...]
  transfers between devices with their start and end apart: 16 -> 59, of which waited for: 15 -> 28; matrix products, arithmetic and copies ran while one was open for 12% -> 24% of each run, Pallas kernels for 0% -> 2%
where the time goes in v1:
time: 605 us; the launch traced here: 598 us
  waiting for transfers between devices  226 us (37%)
  matrix products  170 us (28%)
  other arithmetic  65.7 us (11%)
  starting transfers between devices  57.3 us (9%)
  local copies, waits for them, and re-layouts  37.9 us (6%)
  Pallas kernels  37.7 us (6%)
    ppermute x59, waiting for transfers between devices, exchange(): return lax.ppermute(block, AXES, [(src, src ^ bit) for src in range(32)])  226 us
    dot_general x10, matrix products, dot(): return jnp.dot(left, right, preferred_element_type=f32)  91.2 us
    ppermute x59, starting transfers between devices, exchange(): return lax.ppermute(block, AXES, [(src, src ^ bit) for src in range(32)])  57.3 us
    dot_general x9, matrix products, cols_of(): lax.dot_general(left, right, (((1,), (1,)), ((), ())), preferred_element_...  39.2 us
    dot_general x8, matrix products, rows_of(): lax.dot_general(left, right, (((0,), (0,)), ((), ())), preferred_element_...  34.7 us
    concatenate x2, other arithmetic, assemble(): jnp.concatenate([jnp.concatenate(low, axis=0), jnp.concatenate(high, axis...  29.1 us
    pallas_call x1, Pallas kernels, attend_back_all(): pl.pallas_call(attend_back_kernel, grid=(images, 8), in_specs=[pl.BlockSp...  23.2 us
    pallas_call x1, Pallas kernels, attend(): pl.pallas_call(attend_kernel, grid=(images, 8), in_specs=[pl.BlockSpec((S...  14.5 us
  transfers between devices with their start and end apart: 59, of which 28 were waited for; matrix products, arithmetic and copies ran while one was open for 24% of the time, Pallas kernels for 2%

profile of v1, /device:TPU:0, one launch (start us, length us, event | category | flops | bytes accessed | tf_op | source)
XLA Modules:
  0.0 598.2 jit_solution(17272995004058820866)
XLA Ops:
  2.1 2.9 collective-permute-start.9
  18.2 3.2 fusion.126
  24.2 15.1 %collective-permute-done.17 = bf16[64,2048]{1,0:T(8,128)(2,1)S(1)} collective-permute-done((bf16[64,2048]{1,0:T(8,128)(2,1)}, bf16[64,2048]{1,0:T(8,128)(2,1)S(1)}, u32[]{:S(2)}, u32[]{:S(2)}) %collective-permute-start.17) | collective-permute-done | bytes 262176 | tf_op jit(solution)/shard_map/ppermute | solution.py:249
  47.6 5.5 collective-permute-done.11
  61.9 19.0 %collective-permute-done.13 = bf16[2,128,2048]{2,1,0:T(8,128)(2,1)S(1)} collective-permute-done((bf16[2,128,2048]{2,1,0:T(8,128)(2,1)S(1)}, bf16[2,128,2048]{2,1,0:T(8,128)(2,1)S(1)}, u32[]{:S(2)}, u32[]{:S(2)}) %collective-permute-start.13) | collective-permute-done | bytes 1048608 | tf_op jit(solution)/shard_map/ppermute | solution.py:249
  82.4 21.0 %collective-permute-done.3 = bf16[2,128,2048]{2,1,0:T(8,128)(2,1)S(1)} collective-permute-done((bf16[2,128,2048]{2,1,0:T(8,128)(2,1)S(1)}, bf16[2,128,2048]{2,1,0:T(8,128)(2,1)S(1)}, u32[]{:S(2)}, u32[]{:S(2)}) %collective-permute-start.3) | collective-permute-done | bytes 1048608 | tf_op jit(solution)/shard_map/ppermute | solution.py:249
  104.4 17.3 %collective-permute-done.20 = bf16[2,128,2048]{2,1,0:T(8,128)(2,1)S(1)} collective-permute-done((bf16[2,128,2048]{2,1,0:T(8,128)(2,1)S(1)}, bf16[2,128,2048]{2,1,0:T(8,128)(2,1)S(1)}, u32[]{:S(2)}, u32[]{:S(2)}) %collective-permute-start.20) | collective-permute-done | bytes 1048608 | tf_op jit(solution)/shard_map/ppermute | solution.py:249
  130.5 17.3 %collective-permute-done.7 = bf16[2,256,1024]{2,1,0:T(8,128)(2,1)S(1)} collective-permute-done((bf16[2,256,1024]{2,1,0:T(8,128)(2,1)S(1)}, bf16[2,256,1024]{2,1,0:T(8,128)(2,1)S(1)}, u32[]{:S(2)}, u32[]{:S(2)}) %collective-permute-start.7) | collective-permute-done | bytes 1048608 | tf_op jit(solution)/shard_map/ppermute | solution.py:249
  148.5 3.4 collective-permute-done.21
  153.0 12.5 %collective-permute-done.26 = bf16[2,256,1024]{2,1,0:T(8,128)(2,1)S(1)} collective-permute-done((bf16[2,256,1024]{2,1,0:T(8,128)(2,1)S(1)}, bf16[2,256,1024]{2,1,0:T(8,128)(2,1)S(1)}, u32[]{:S(2)}, u32[]{:S(2)}) %collective-permute-start.26) | collective-permute-done | bytes 1048608 | tf_op jit(solution)/shard_map/ppermute | solution.py:249
  168.2 13.0 %fusion.39 = bf16[1024,1536]{1,0:T(8,128)(2,1)S(1)} fusion(bf16[256,1024]{1,0:T(8,128)(2,1)S(1)} %get-tuple-element.138, bf16[256,1024]{1,0:T(8,128)(2,1)S(1)} %get-tuple-element.134, bf16[256,1024]{1,0:T(8,128)(2,1)S(1)} %get-tuple-element.137, bf16[256,1024]{1,0:T(8,128)(2,1)S(1)} %get-tuple-element.92, bf16[256,1024]{1,0:T(8,128)(2,1)S(1)} %get-tuple-element.136, ...), kind=kLoop, calls=%fused_computation.93 | loop fusion | flops 25165824 | bytes 7340032 | tf_op jit(solution)/shard_map/concatenate | solution.py:275
  183.4 14.7 %add_convert_fusion.1 = bf16[584,1536]{1,0:T(8,128)(2,1)S(1)} fusion(bf16[584,1024]{1,0:T(8,128)(2,1)S(1)} %add_convert_fusion.4, f32[1536]{0:T(1024)S(1)} %get-tuple-element.164, bf16[256,1024]{1,0:T(8,128)(2,1)S(1)} %get-tuple-element.93, bf16[256,1024]{1,0:T(8,128)(2,1)S(1)} %get-tuple-element.133, bf16[256,1024]{1,0:T(8,128)(2,1)S(1)} %get-tuple-element.94, ...), kind=kOutput, calls=%fused_computation.87 | convolution fusion | flops 1864065024 | bytes 7190528 | tf_op jit(solution)/shard_map/dot_general | solution.py:440
  198.5 14.5 %shard_map.254 = (bf16[584,1024]{1,0:T(8,128)(2,1)S(1)}, f32[8,2,584]{2,1,0:T(2,128)S(1)}) custom-call(bf16[584,3072]{1,0:T(8,128)(2,1)S(1)} %pad_maximum_fusion.2.q_ref.k_ref.v_ref, bf16[584,3072]{1,0:T(8,128)(2,1)S(1)} %pad_maximum_fusion.2.q_ref.k_ref.v_ref, bf16[584,3072]{1,0:T(8,128)(2,1)S(1)} %pad_maximum_fusion.2.q_ref.k_ref.v_ref), custom_call_target="tpu_custom_call" | custom-call | flops 14000000000 | bytes 5000000 | tf_op jit(solution)/shard_map/pallas_call | solution.py:340
  222.8 16.1 %maximum_maximum_fusion.3 = bf16[1024,2048]{1,0:T(8,128)(2,1)S(1)} fusion(bf16[256,1024]{1,0:T(8,128)(2,1)S(1)} %get-tuple-element.130, bf16[256,1024]{1,0:T(8,128)(2,1)S(1)} %get-tuple-element.129, bf16[256,1024]{1,0:T(8,128)(2,1)S(1)} %get-tuple-element.128, bf16[256,1024]{1,0:T(8,128)(2,1)S(1)} %get-tuple-element.127, ...), kind=kLoop, calls=%fused_computation.75 | loop fusion | flops 33554432 | bytes 8388608 | tf_op jit(solution)/shard_map/concatenate | solution.py:275
  238.9 4.6 multiply_convert_fusion.2
  244.9 5.3 convert_bitcast_fusion
  252.4 5.8 fusion.99
  258.2 22.3 %convert_reduce_fusion = (f32[2048]{0:T(1024)}, bf16[584,2048]{1,0:T(8,128)(2,1)}) fusion(f32[584,2048]{1,0:T(8,128)} %get-tuple-element.172, f32[2048]{0:T(1024)S(1)} %bitcast.307, bf16[584,1024]{1,0:T(8,128)(2,1)S(1)} %convolution_convert_fusion.3, bf16[256,1024]{1,0:T(8,128)(2,1)S(1)} %get-tuple-element.126, ...), kind=kOutput, calls=%fused_computation.37 | convolution fusion | flops 2500966400 | bytes 12582912 | tf_op jit(solution)/shard_map/dot_general | solution.py:440
  280.5 5.9 fusion.128
  286.5 5.1 convert_bitcast_fusion.2
  291.8 19.8 %multiply_convert_fusion.3 = (bf16[584,2048]{1,0:T(8,128)(2,1)}, f32[584,2048]{1,0:T(8,128)}) fusion(f32[2048]{0:T(1024)S(1)} %bitcast.304, bf16[584,1024]{1,0:T(8,128)(2,1)S(1)} %add_convert_fusion.3, bf16[256,1024]{1,0:T(8,128)(2,1)S(1)} %copy-done.69, bf16[256,1024]{1,0:T(8,128)(2,1)S(1)} %copy-done.70, bf16[256,1024]{1,0:T(8,128)(2,1)S(1)} %copy-done.53, ...), kind=kOutput, calls=%fused_computation.43 | convolution fusion | flops 2490204160 | bytes 12574720 | tf_op jit(solution)/shard_map/dot_general | solution.py:440
  311.6 21.5 %convert_reduce_fusion.1 = (f32[2048]{0:T(1024)}, bf16[584,2048]{1,0:T(8,128)(2,1)}) fusion(f32[584,2048]{1,0:T(8,128)} %get-tuple-element.174, f32[2048]{0:T(1024)S(1)} %bitcast.305, bf16[584,1024]{1,0:T(8,128)(2,1)S(1)} %convolution_convert_fusion.3, bf16[256,1024]{1,0:T(8,128)(2,1)S(1)} %get-tuple-element.73, ...), kind=kOutput, calls=%fused_computation.38 | convolution fusion | flops 2500966400 | bytes 12582912 | tf_op jit(solution)/shard_map/dot_general | solution.py:440
  333.1 5.7 multiply_reduce_fusion
  342.9 23.2 %shard_map.255 = (bf16[584,1024]{1,0:T(8,128)(2,1)S(1)}, bf16[584,1024]{1,0:T(8,128)(2,1)S(1)}, bf16[584,1024]{1,0:T(8,128)(2,1)S(1)}) custom-call(bf16[584,3072]{1,0:T(8,128)(2,1)S(1)} %pad_maximum_fusion.2.q_ref.k_ref.v_ref, bf16[584,3072]{1,0:T(8,128)(2,1)S(1)} %pad_maximum_fusion.2.q_ref.k_ref.v_ref, ...), custom_call_target="tpu_custom_call" | custom-call | flops 28000000000 | bytes 9000000 | tf_op jit(solution)/shard_map/pallas_call | solution.py:393
  372.3 3.5 fusion.54
  375.8 4.4 fusion.38
  380.2 5.3 convert_bitcast_fusion.3
  385.8 6.3 %fusion.37 = bf16[1,1024,1536]{2,1,0:T(8,128)(2,1)} fusion(bf16[584,1024]{1,0:T(8,128)(2,1)} %copy-done.20, bf16[584,512]{1,0:T(8,128)(2,1)} %get-tuple-element.101, bf16[584,512]{1,0:T(8,128)(2,1)} %get-tuple-element.99, bf16[584,512]{1,0:T(8,128)(2,1)} %get-tuple-element.97), kind=kOutput, calls=%fused_computation.90 | convolution fusion | flops 1844060160 | bytes 6135808 | tf_op jit(solution)/shard_map/dot_general | solution.py:434
  392.2 4.0 multiply_reduce_fusion.1
  396.3 3.3 fusion.101
  402.3 5.2 convert_bitcast_fusion.1
  407.5 9.5 %convolution_convert_fusion.4 = bf16[584,1024]{1,0:T(8,128)(2,1)} fusion(f32[584,1024]{1,0:T(8,128)} %copy-done.4, f32[584,1024]{1,0:T(8,128)} %fusion.99, bf16[584,2048]{1,0:T(8,128)(2,1)} %get-tuple-element.173, f32[584]{0:T(1024)} %get-tuple-element.65, f32[1024]{0:T(1024)S(1)} %bitcast.325, bf16[256,1024]{1,0:T(8,128)(2,1)} %copy-done.66, ...), kind=kOutput, calls=%fused_computation.137 | convolution fusion | flops 3787898880 | bytes 12591396 | tf_op jit(solution)/shard_map/dot_general | solution.py:437
  417.0 5.7 maximum_maximum_fusion
  431.6 3.1 collective-permute-done.36
  442.8 3.9 collective-permute-start.39
  448.3 2.9 convolution_convert_fusion.2
  456.8 3.8 fusion.25
  464.9 2.9 slice_add_fusion
  476.9 11.1 %collective-permute-done.53 = bf16[2,256,1024]{2,1,0:T(8,128)(2,1)S(1)} collective-permute-done((bf16[2,256,1024]{2,1,0:T(8,128)(2,1)}, bf16[2,256,1024]{2,1,0:T(8,128)(2,1)S(1)}, u32[]{:S(2)}, u32[]{:S(2)}) %collective-permute-start.53) | collective-permute-done | bytes 1048608 | tf_op jit(solution)/shard_map/ppermute | solution.py:249
  489.4 6.5 %collective-permute-done.54 = bf16[512,1024]{1,0:T(8,128)(2,1)S(1)} collective-permute-done((bf16[512,1024]{1,0:T(8,128)(2,1)S(1)}, bf16[512,1024]{1,0:T(8,128)(2,1)S(1)}, u32[]{:S(2)}, u32[]{:S(2)}) %collective-permute-start.54) | collective-permute-done | bytes 1048608 | tf_op jit(solution)/shard_map/ppermute | solution.py:249
  497.0 13.4 %collective-permute-done.29 = bf16[2,256,1024]{2,1,0:T(8,128)(2,1)S(1)} collective-permute-done((bf16[2,256,1024]{2,1,0:T(8,128)(2,1)S(1)}, bf16[2,256,1024]{2,1,0:T(8,128)(2,1)S(1)}, u32[]{:S(2)}, u32[]{:S(2)}) %collective-permute-start.29) | collective-permute-done | bytes 1048608 | tf_op jit(solution)/shard_map/ppermute | solution.py:249
  510.6 7.7 %collective-permute-done.30 = bf16[512,1024]{1,0:T(8,128)(2,1)S(1)} collective-permute-done((bf16[512,1024]{1,0:T(8,128)(2,1)S(1)}, bf16[512,1024]{1,0:T(8,128)(2,1)S(1)}, u32[]{:S(2)}, u32[]{:S(2)}) %collective-permute-start.30) | collective-permute-done | bytes 1048608 | tf_op jit(solution)/shard_map/ppermute | solution.py:249
  519.5 10.6 %collective-permute-done.46 = bf16[2,256,1024]{2,1,0:T(8,128)(2,1)S(1)} collective-permute-done((bf16[2,256,1024]{2,1,0:T(8,128)(2,1)S(1)}, bf16[2,256,1024]{2,1,0:T(8,128)(2,1)S(1)}, u32[]{:S(2)}, u32[]{:S(2)}) %collective-permute-start.46) | collective-permute-done | bytes 1048608 | tf_op jit(solution)/shard_map/ppermute | solution.py:249
  530.2 7.8 %collective-permute-done.47 = bf16[512,1024]{1,0:T(8,128)(2,1)S(1)} collective-permute-done((bf16[512,1024]{1,0:T(8,128)(2,1)S(1)}, bf16[512,1024]{1,0:T(8,128)(2,1)S(1)}, u32[]{:S(2)}, u32[]{:S(2)}) %collective-permute-start.47) | collective-permute-done | bytes 1048608 | tf_op jit(solution)/shard_map/ppermute | solution.py:249
  543.6 17.1 %collective-permute-done.48 = bf16[2,128,2048]{2,1,0:T(8,128)(2,1)S(1)} collective-permute-done((bf16[2,128,2048]{2,1,0:T(8,128)(2,1)S(1)}, bf16[2,128,2048]{2,1,0:T(8,128)(2,1)S(1)}, u32[]{:S(2)}, u32[]{:S(2)}) %collective-permute-start.48) | collective-permute-done | bytes 1048608 | tf_op jit(solution)/shard_map/ppermute | solution.py:249
  570.5 15.3 %collective-permute-done.58 = bf16[64,2048]{1,0:T(8,128)(2,1)S(1)} collective-permute-done((bf16[64,2048]{1,0:T(8,128)(2,1)S(1)}, bf16[64,2048]{1,0:T(8,128)(2,1)S(1)}, u32[]{:S(2)}, u32[]{:S(2)}) %collective-permute-start.58) | collective-permute-done | bytes 262176 | tf_op jit(solution)/shard_map/ppermute | solution.py:249
  586.6 4.8 collective-permute-done.34
  593.3 3.6 collective-permute-done.51
  (450 shorter events, 138.6 us)
Async XLA Ops:
  2.1 21.9 %collective-permute-start.9 = (f32[1,3072]{1,0:T(1,128)S(1)}, f32[1,3072]{1,0:T(1,128)S(1)}, u32[]{:S(2)}, u32[]{:S(2)}) collective-permute-start(f32[1,3072]{1,0:T(1,128)S(1)} %bitcast.295), channel_id=1, source_target_pairs={{0,1},{1,0},{2,3},{3,2},{4,5},{5,4},{6,7},{7,6},{8,9},{9,8},{10,11... | collective-permute-start | bytes 36872 | tf_op jit(solution)/shard_map/ppermute | solution.py:249
  6.9 39.0 %collective-permute-start = (bf16[64,2048]{1,0:T(8,128)(2,1)S(1)}, bf16[64,2048]{1,0:T(8,128)(2,1)S(1)}, u32[]{:S(2)}, u32[]{:S(2)}) collective-permute-start(bf16[64,2048]{1,0:T(8,128)(2,1)S(1)} %pad_maximum_fusion.42), channel_id=1, source_target_pairs={{0,16},{1,17},{2,18},{3,19},{4,20},{5,21},{6,22},{7,23},{8,24},{9,... | collective-permute-start | bytes 786440 | tf_op jit(solution)/shard_map/ppermute | solution.py:249
  9.5 29.7 %collective-permute-start.17 = (bf16[64,2048]{1,0:T(8,128)(2,1)}, bf16[64,2048]{1,0:T(8,128)(2,1)S(1)}, u32[]{:S(2)}, u32[]{:S(2)}) collective-permute-start(bf16[64,2048]{1,0:T(8,128)(2,1)} %bitcast.283), channel_id=1, source_target_pairs={{0,16},{1,17},{2,18},{3,19},{4,20},{5,21},{6,22},{7,23},{8,24},{9,... | collective-permute-start | bytes 786440 | tf_op jit(solution)/shard_map/ppermute | solution.py:249
  9.9 33.8 %collective-permute-start.10 = (bf16[64,2048]{1,0:T(8,128)(2,1)}, bf16[64,2048]{1,0:T(8,128)(2,1)S(1)}, u32[]{:S(2)}, u32[]{:S(2)}) collective-permute-start(bf16[64,2048]{1,0:T(8,128)(2,1)} %param.21), channel_id=1, source_target_pairs={{0,16},{1,17},{2,18},{3,19},{4,20},{5,21},{6,22},{7,23},{8,24},{9,... | collective-permute-start | bytes 786440 | tf_op jit(solution)/shard_map/ppermute | solution.py:249
  39.3 21.1 %collective-permute-start.18 = (bf16[128,1024]{1,0:T(8,128)(2,1)S(1)}, bf16[128,1024]{1,0:T(8,128)(2,1)S(1)}, u32[]{:S(2)}, u32[]{:S(2)}) collective-permute-start(bf16[128,1024]{1,0:T(8,128)(2,1)S(1)} %get-tuple-element.139), channel_id=1, source_target_pairs={{0,1},{1,0},{2,3},{3,2},{4,5},{5,4},{6,7},{7,6},{8,9},{9,8},{10,11... | collective-permute-start | bytes 786440 | tf_op jit(solution)/shard_map/ppermute | solution.py:249
  39.8 20.6 %collective-permute-start.19 = (bf16[128,1024]{1,0:T(8,128)(2,1)S(1)}, bf16[128,1024]{1,0:T(8,128)(2,1)S(1)}, u32[]{:S(2)}, u32[]{:S(2)}) collective-permute-start(bf16[128,1024]{1,0:T(8,128)(2,1)S(1)} %get-tuple-element.140), channel_id=1, source_target_pairs={{0,4},{1,5},{2,6},{3,7},{4,0},{5,1},{6,2},{7,3},{8,12},{9,13},{10,... | collective-permute-start | bytes 786440 | tf_op jit(solution)/shard_map/ppermute | solution.py:249
  43.8 9.3 %collective-permute-start.11 = (bf16[128,1024]{1,0:T(8,128)(2,1)S(1)}, bf16[128,1024]{1,0:T(8,128)(2,1)S(1)}, u32[]{:S(2)}, u32[]{:S(2)}) collective-permute-start(bf16[128,1024]{1,0:T(8,128)(2,1)S(1)} %get-tuple-element.141), channel_id=1, source_target_pairs={{0,1},{1,0},{2,3},{3,2},{4,5},{5,4},{6,7},{7,6},{8,9},{9,8},{10,11... | collective-permute-start | bytes 786440 | tf_op jit(solution)/shard_map/ppermute | solution.py:249
  44.3 10.3 %collective-permute-start.12 = (bf16[128,1024]{1,0:T(8,128)(2,1)S(1)}, bf16[128,1024]{1,0:T(8,128)(2,1)S(1)}, u32[]{:S(2)}, u32[]{:S(2)}) collective-permute-start(bf16[128,1024]{1,0:T(8,128)(2,1)S(1)} %get-tuple-element.142), channel_id=1, source_target_pairs={{0,4},{1,5},{2,6},{3,7},{4,0},{5,1},{6,2},{7,3},{8,12},{9,13},{10,... | collective-permute-start | bytes 786440 | tf_op jit(solution)/shard_map/ppermute | solution.py:249
  46.0 11.0 %collective-permute-start.1 = (bf16[128,1024]{1,0:T(8,128)(2,1)S(1)}, bf16[128,1024]{1,0:T(8,128)(2,1)S(1)}, u32[]{:S(2)}, u32[]{:S(2)}) collective-permute-start(bf16[128,1024]{1,0:T(8,128)(2,1)S(1)} %get-tuple-element.143), channel_id=1, source_target_pairs={{0,1},{1,0},{2,3},{3,2},{4,5},{5,4},{6,7},{7,6},{8,9},{9,8},{10,11... | collective-permute-start | bytes 786440 | tf_op jit(solution)/shard_map/ppermute | solution.py:249
  54.7 26.2 %collective-permute-start.13 = (bf16[2,128,2048]{2,1,0:T(8,128)(2,1)S(1)}, bf16[2,128,2048]{2,1,0:T(8,128)(2,1)S(1)}, u32[]{:S(2)}, u32[]{:S(2)}) collective-permute-start(bf16[2,128,2048]{2,1,0:T(8,128)(2,1)S(1)} %pad_maximum_fusion.31), channel_id=1, source_target_pairs={{0,8},{1,9},{2,10},{3,11},{4,12},{5,13},{6,14},{7,15},{8,0},{9,1},... | collective-permute-start | bytes 3145736 | tf_op jit(solution)/shard_map/ppermute | solution.py:249
  59.6 43.8 %collective-permute-start.3 = (bf16[2,128,2048]{2,1,0:T(8,128)(2,1)S(1)}, bf16[2,128,2048]{2,1,0:T(8,128)(2,1)S(1)}, u32[]{:S(2)}, u32[]{:S(2)}) collective-permute-start(bf16[2,128,2048]{2,1,0:T(8,128)(2,1)S(1)} %pad_maximum_fusion.30), channel_id=1, source_target_pairs={{0,8},{1,9},{2,10},{3,11},{4,12},{5,13},{6,14},{7,15},{8,0},{9,1},... | collective-permute-start | bytes 3145736 | tf_op jit(solution)/shard_map/ppermute | solution.py:249
  60.6 61.1 %collective-permute-start.20 = (bf16[2,128,2048]{2,1,0:T(8,128)(2,1)S(1)}, bf16[2,128,2048]{2,1,0:T(8,128)(2,1)S(1)}, u32[]{:S(2)}, u32[]{:S(2)}) collective-permute-start(bf16[2,128,2048]{2,1,0:T(8,128)(2,1)S(1)} %pad_maximum_fusion.32), channel_id=1, source_target_pairs={{0,8},{1,9},{2,10},{3,11},{4,12},{5,13},{6,14},{7,15},{8,0},{9,1},... | collective-permute-start | bytes 3145736 | tf_op jit(solution)/shard_map/ppermute | solution.py:249
  81.3 44.2 %collective-permute-start.14 = (bf16[2,256,1024]{2,1,0:T(8,128)(2,1)S(1)}, bf16[2,256,1024]{2,1,0:T(8,128)(2,1)S(1)}, u32[]{:S(2)}, u32[]{:S(2)}) collective-permute-start(bf16[2,256,1024]{2,1,0:T(8,128)(2,1)S(1)} %get-tuple-element.85), channel_id=1, source_target_pairs={{0,4},{1,5},{2,6},{3,7},{4,0},{5,1},{6,2},{7,3},{8,12},{9,13},{10,... | collective-permute-start | bytes 3145736 | tf_op jit(solution)/shard_map/ppermute | solution.py:249
  81.9 66.0 %collective-permute-start.24 = (bf16[2,256,1024]{2,1,0:T(8,128)(2,1)S(1)}, bf16[2,256,1024]{2,1,0:T(8,128)(2,1)S(1)}, u32[]{:S(2)}, u32[]{:S(2)}) collective-permute-start(bf16[2,256,1024]{2,1,0:T(8,128)(2,1)S(1)} %get-tuple-element.86), channel_id=1, source_target_pairs={{0,1},{1,0},{2,3},{3,2},{4,5},{5,4},{6,7},{7,6},{8,9},{9,8},{10,11... | collective-permute-start | bytes 3145736 | tf_op jit(solution)/shard_map/ppermute | solution.py:249
  103.6 63.8 %collective-permute-start.5 = (bf16[2,256,2048]{2,1,0:T(8,128)(2,1)S(1)}, bf16[2,256,2048]{2,1,0:T(8,128)(2,1)S(1)}, u32[]{:S(2)}, u32[]{:S(2)}) collective-permute-start(bf16[2,256,2048]{2,1,0:T(8,128)(2,1)S(1)} %pad_maximum_fusion.15), channel_id=1, source_target_pairs={{0,2},{1,3},{2,0},{3,1},{4,6},{5,7},{6,4},{7,5},{8,10},{9,11},{10,... | collective-permute-start | bytes 6291464 | tf_op jit(solution)/shard_map/ppermute | solution.py:249
  103.8 26.0 %collective-permute-start.4 = (bf16[2,256,1024]{2,1,0:T(8,128)(2,1)S(1)}, bf16[2,256,1024]{2,1,0:T(8,128)(2,1)S(1)}, u32[]{:S(2)}, u32[]{:S(2)}) collective-permute-start(bf16[2,256,1024]{2,1,0:T(8,128)(2,1)S(1)} %get-tuple-element.95), channel_id=1, source_target_pairs={{0,4},{1,5},{2,6},{3,7},{4,0},{5,1},{6,2},{7,3},{8,12},{9,13},{10,... | collective-permute-start | bytes 3145736 | tf_op jit(solution)/shard_map/ppermute | solution.py:249
  121.7 26.1 %collective-permute-start.7 = (bf16[2,256,1024]{2,1,0:T(8,128)(2,1)S(1)}, bf16[2,256,1024]{2,1,0:T(8,128)(2,1)S(1)}, u32[]{:S(2)}, u32[]{:S(2)}) collective-permute-start(bf16[2,256,1024]{2,1,0:T(8,128)(2,1)S(1)} %get-tuple-element.96), channel_id=1, source_target_pairs={{0,1},{1,0},{2,3},{3,2},{4,5},{5,4},{6,7},{7,6},{8,9},{9,8},{10,11... | collective-permute-start | bytes 3145736 | tf_op jit(solution)/shard_map/ppermute | solution.py:249
  125.5 26.4 %collective-permute-start.21 = (bf16[2,256,1024]{2,1,0:T(8,128)(2,1)S(1)}, bf16[2,256,1024]{2,1,0:T(8,128)(2,1)S(1)}, u32[]{:S(2)}, u32[]{:S(2)}) collective-permute-start(bf16[2,256,1024]{2,1,0:T(8,128)(2,1)S(1)} %get-tuple-element.83), channel_id=1, source_target_pairs={{0,4},{1,5},{2,6},{3,7},{4,0},{5,1},{6,2},{7,3},{8,12},{9,13},{10,... | collective-permute-start | bytes 3145736 | tf_op jit(solution)/shard_map/ppermute | solution.py:249
  129.9 35.7 %collective-permute-start.26 = (bf16[2,256,1024]{2,1,0:T(8,128)(2,1)S(1)}, bf16[2,256,1024]{2,1,0:T(8,128)(2,1)S(1)}, u32[]{:S(2)}, u32[]{:S(2)}) collective-permute-start(bf16[2,256,1024]{2,1,0:T(8,128)(2,1)S(1)} %get-tuple-element.84), channel_id=1, source_target_pairs={{0,1},{1,0},{2,3},{3,2},{4,5},{5,4},{6,7},{7,6},{8,9},{9,8},{10,11... | collective-permute-start | bytes 3145736 | tf_op jit(solution)/shard_map/ppermute | solution.py:249
  147.8 18.8 %collective-permute-start.6 = (bf16[2,256,1024]{2,1,0:T(8,128)(2,1)S(1)}, bf16[2,256,1024]{2,1,0:T(8,128)(2,1)S(1)}, u32[]{:S(2)}, u32[]{:S(2)}) collective-permute-start(bf16[2,256,1024]{2,1,0:T(8,128)(2,1)S(1)} %collective-permute-done.4), channel_id=1, source_target_pairs={{0,2},{1,3},{2,0},{3,1},{4,6},{5,7},{6,4},{7,5},{8,10},{9,11},{10,... | collective-permute-start | bytes 3145736 | tf_op jit(solution)/shard_map/ppermute | solution.py:249
  147.9 19.3 %collective-permute-start.8 = (bf16[2,256,1024]{2,1,0:T(8,128)(2,1)S(1)}, bf16[2,256,1024]{2,1,0:T(8,128)(2,1)S(1)}, u32[]{:S(2)}, u32[]{:S(2)}) collective-permute-start(bf16[2,256,1024]{2,1,0:T(8,128)(2,1)S(1)} %collective-permute-done.7), channel_id=1, source_target_pairs={{0,2},{1,3},{2,0},{3,1},{4,6},{5,7},{6,4},{7,5},{8,10},{9,11},{10,... | collective-permute-start | bytes 3145736 | tf_op jit(solution)/shard_map/ppermute | solution.py:249
  151.9 69.7 %collective-permute-start.15 = (bf16[2,256,2048]{2,1,0:T(8,128)(2,1)S(1)}, bf16[2,256,2048]{2,1,0:T(8,128)(2,1)S(1)}, u32[]{:S(2)}, u32[]{:S(2)}) collective-permute-start(bf16[2,256,2048]{2,1,0:T(8,128)(2,1)S(1)} %pad_maximum_fusion.16), channel_id=1, source_target_pairs={{0,2},{1,3},{2,0},{3,1},{4,6},{5,7},{6,4},{7,5},{8,10},{9,11},{10,... | collective-permute-start | bytes 6291464 | tf_op jit(solution)/shard_map/ppermute | solution.py:249
  165.5 49.8 %collective-permute-start.16 = (bf16[2,256,1024]{2,1,0:T(8,128)(2,1)S(1)}, bf16[2,256,1024]{2,1,0:T(8,128)(2,1)}, u32[]{:S(2)}, u32[]{:S(2)}) collective-permute-start(bf16[2,256,1024]{2,1,0:T(8,128)(2,1)S(1)} %collective-permute-done.14), channel_id=1, source_target_pairs={{0,2},{1,3},{2,0},{3,1},{4,6},{5,7},{6,4},{7,5},{8,10},{9,11},{10,... | collective-permute-start | bytes 3145736 | tf_op jit(solution)/shard_map/ppermute | solution.py:249
  166.6 50.5 %collective-permute-start.25 = (bf16[2,256,1024]{2,1,0:T(8,128)(2,1)S(1)}, bf16[2,256,1024]{2,1,0:T(8,128)(2,1)}, u32[]{:S(2)}, u32[]{:S(2)}) collective-permute-start(bf16[2,256,1024]{2,1,0:T(8,128)(2,1)S(1)} %collective-permute-done.24), channel_id=1, source_target_pairs={{0,2},{1,3},{2,0},{3,1},{4,6},{5,7},{6,4},{7,5},{8,10},{9,11},{10,... | collective-permute-start | bytes 3145736 | tf_op jit(solution)/shard_map/ppermute | solution.py:249
  167.2 51.1 %collective-permute-start.23 = (bf16[2,256,1024]{2,1,0:T(8,128)(2,1)S(1)}, bf16[2,256,1024]{2,1,0:T(8,128)(2,1)}, u32[]{:S(2)}, u32[]{:S(2)}) collective-permute-start(bf16[2,256,1024]{2,1,0:T(8,128)(2,1)S(1)} %collective-permute-done.21), channel_id=1, source_target_pairs={{0,2},{1,3},{2,0},{3,1},{4,6},{5,7},{6,4},{7,5},{8,10},{9,11},{10,... | collective-permute-start | bytes 3145736 | tf_op jit(solution)/shard_map/ppermute | solution.py:249
  167.4 52.3 %collective-permute-start.27 = (bf16[2,256,1024]{2,1,0:T(8,128)(2,1)S(1)}, bf16[2,256,1024]{2,1,0:T(8,128)(2,1)}, u32[]{:S(2)}, u32[]{:S(2)}) collective-permute-start(bf16[2,256,1024]{2,1,0:T(8,128)(2,1)S(1)} %collective-permute-done.26), channel_id=1, source_target_pairs={{0,2},{1,3},{2,0},{3,1},{4,6},{5,7},{6,4},{7,5},{8,10},{9,11},{10,... | collective-permute-start | bytes 3145736 | tf_op jit(solution)/shard_map/ppermute | solution.py:249
  215.4 34.8 %collective-permute-start.22 = (bf16[2,256,2048]{2,1,0:T(8,128)(2,1)S(1)}, bf16[2,256,2048]{2,1,0:T(8,128)(2,1)S(1)}, u32[]{:S(2)}, u32[]{:S(2)}) collective-permute-start(bf16[2,256,2048]{2,1,0:T(8,128)(2,1)S(1)} %pad_maximum_fusion.17), channel_id=1, source_target_pairs={{0,2},{1,3},{2,0},{3,1},{4,6},{5,7},{6,4},{7,5},{8,10},{9,11},{10,... | collective-permute-start | bytes 6291464 | tf_op jit(solution)/shard_map/ppermute | solution.py:249
  400.3 27.8 %collective-permute-start.35 = (f32[1,3072]{1,0:T(1,128)}, f32[1,3072]{1,0:T(1,128)}, u32[]{:S(2)}, u32[]{:S(2)}) collective-permute-start(f32[1,3072]{1,0:T(1,128)} %slice.649), channel_id=1, source_target_pairs={{0,1},{1,0},{2,3},{3,2},{4,5},{5,4},{6,7},{7,6},{8,9},{9,8},{10,11... | collective-permute-start | bytes 36872 | tf_op jit(solution)/shard_map/ppermute | solution.py:249
  400.8 34.6 %collective-permute-start.40 = (f32[6,1024]{1,0:T(8,128)S(1)}, f32[6,1024]{1,0:T(8,128)S(1)}, u32[]{:S(2)}, u32[]{:S(2)}) collective-permute-start(f32[6,1024]{1,0:T(8,128)S(1)} %fusion.101), channel_id=1, source_target_pairs={{0,1},{1,0},{2,3},{3,2},{4,5},{5,4},{6,7},{7,6},{8,9},{9,8},{10,11... | collective-permute-start | bytes 73736 | tf_op jit(solution)/shard_map/ppermute | solution.py:249
  427.5 29.2 %collective-permute-start.52 = (bf16[2,512,2048]{2,1,0:T(8,128)(2,1)}, bf16[2,512,2048]{2,1,0:T(8,128)(2,1)}, u32[]{:S(2)}, u32[]{:S(2)}) collective-permute-start(bf16[2,512,2048]{2,1,0:T(8,128)(2,1)} %pad_maximum_fusion), channel_id=1, source_target_pairs={{0,2},{1,3},{2,0},{3,1},{4,6},{5,7},{6,4},{7,5},{8,10},{9,11},{10,... | collective-permute-start | bytes 12582920 | tf_op jit(solution)/shard_map/ppermute | solution.py:249
  427.5 36.3 %collective-permute-start.28 = (bf16[2,512,2048]{2,1,0:T(8,128)(2,1)}, bf16[2,512,2048]{2,1,0:T(8,128)(2,1)}, u32[]{:S(2)}, u32[]{:S(2)}) collective-permute-start(bf16[2,512,2048]{2,1,0:T(8,128)(2,1)} %slice.634), channel_id=1, source_target_pairs={{0,2},{1,3},{2,0},{3,1},{4,6},{5,7},{6,4},{7,5},{8,10},{9,11},{10,... | collective-permute-start | bytes 12582920 | tf_op jit(solution)/shard_map/ppermute | solution.py:249
  442.1 30.6 %collective-permute-start.45 = (bf16[2,512,2048]{2,1,0:T(8,128)(2,1)}, bf16[2,512,2048]{2,1,0:T(8,128)(2,1)}, u32[]{:S(2)}, u32[]{:S(2)}) collective-permute-start(bf16[2,512,2048]{2,1,0:T(8,128)(2,1)} %pad_maximum_fusion.1), channel_id=1, source_target_pairs={{0,2},{1,3},{2,0},{3,1},{4,6},{5,7},{6,4},{7,5},{8,10},{9,11},{10,... | collective-permute-start | bytes 12582920 | tf_op jit(solution)/shard_map/ppermute | solution.py:249
  461.7 26.3 %collective-permute-start.53 = (bf16[2,256,1024]{2,1,0:T(8,128)(2,1)}, bf16[2,256,1024]{2,1,0:T(8,128)(2,1)S(1)}, u32[]{:S(2)}, u32[]{:S(2)}) collective-permute-start(bf16[2,256,1024]{2,1,0:T(8,128)(2,1)} %slice.671), channel_id=1, source_target_pairs={{0,4},{1,5},{2,6},{3,7},{4,0},{5,1},{6,2},{7,3},{8,12},{9,13},{10,... | collective-permute-start | bytes 3145736 | tf_op jit(solution)/shard_map/ppermute | solution.py:249
  469.8 26.1 %collective-permute-start.54 = (bf16[512,1024]{1,0:T(8,128)(2,1)S(1)}, bf16[512,1024]{1,0:T(8,128)(2,1)S(1)}, u32[]{:S(2)}, u32[]{:S(2)}) collective-permute-start(bf16[512,1024]{1,0:T(8,128)(2,1)S(1)} %copy-done.25), channel_id=1, source_target_pairs={{0,1},{1,0},{2,3},{3,2},{4,5},{5,4},{6,7},{7,6},{8,9},{9,8},{10,11... | collective-permute-start | bytes 3145736 | tf_op jit(solution)/shard_map/ppermute | solution.py:249
  471.1 39.4 %collective-permute-start.29 = (bf16[2,256,1024]{2,1,0:T(8,128)(2,1)S(1)}, bf16[2,256,1024]{2,1,0:T(8,128)(2,1)S(1)}, u32[]{:S(2)}, u32[]{:S(2)}) collective-permute-start(bf16[2,256,1024]{2,1,0:T(8,128)(2,1)S(1)} %slice.636), channel_id=1, source_target_pairs={{0,4},{1,5},{2,6},{3,7},{4,0},{5,1},{6,2},{7,3},{8,12},{9,13},{10,... | collective-permute-start | bytes 3145736 | tf_op jit(solution)/shard_map/ppermute | solution.py:249
  472.1 46.2 %collective-permute-start.30 = (bf16[512,1024]{1,0:T(8,128)(2,1)S(1)}, bf16[512,1024]{1,0:T(8,128)(2,1)S(1)}, u32[]{:S(2)}, u32[]{:S(2)}) collective-permute-start(bf16[512,1024]{1,0:T(8,128)(2,1)S(1)} %slice_bitcast_fusion.4), channel_id=1, source_target_pairs={{0,1},{1,0},{2,3},{3,2},{4,5},{5,4},{6,7},{7,6},{8,9},{9,8},{10,11... | collective-permute-start | bytes 3145736 | tf_op jit(solution)/shard_map/ppermute | solution.py:249
  475.7 54.4 %collective-permute-start.46 = (bf16[2,256,1024]{2,1,0:T(8,128)(2,1)S(1)}, bf16[2,256,1024]{2,1,0:T(8,128)(2,1)S(1)}, u32[]{:S(2)}, u32[]{:S(2)}) collective-permute-start(bf16[2,256,1024]{2,1,0:T(8,128)(2,1)S(1)} %slice.656), channel_id=1, source_target_pairs={{0,4},{1,5},{2,6},{3,7},{4,0},{5,1},{6,2},{7,3},{8,12},{9,13},{10,... | collective-permute-start | bytes 3145736 | tf_op jit(solution)/shard_map/ppermute | solution.py:249
  488.0 50.0 %collective-permute-start.47 = (bf16[512,1024]{1,0:T(8,128)(2,1)S(1)}, bf16[512,1024]{1,0:T(8,128)(2,1)S(1)}, u32[]{:S(2)}, u32[]{:S(2)}) collective-permute-start(bf16[512,1024]{1,0:T(8,128)(2,1)S(1)} %slice_bitcast_fusion.2), channel_id=1, source_target_pairs={{0,1},{1,0},{2,3},{3,2},{4,5},{5,4},{6,7},{7,6},{8,9},{9,8},{10,11... | collective-permute-start | bytes 3145736 | tf_op jit(solution)/shard_map/ppermute | solution.py:249
  496.1 42.5 %collective-permute-start.55 = (bf16[2,128,2048]{2,1,0:T(8,128)(2,1)S(1)}, bf16[2,128,2048]{2,1,0:T(8,128)(2,1)S(1)}, u32[]{:S(2)}, u32[]{:S(2)}) collective-permute-start(bf16[2,128,2048]{2,1,0:T(8,128)(2,1)S(1)} %pad_maximum_fusion.21), channel_id=1, source_target_pairs={{0,8},{1,9},{2,10},{3,11},{4,12},{5,13},{6,14},{7,15},{8,0},{9,1},... | collective-permute-start | bytes 3145736 | tf_op jit(solution)/shard_map/ppermute | solution.py:249
  518.6 22.6 %collective-permute-start.31 = (bf16[2,128,2048]{2,1,0:T(8,128)(2,1)S(1)}, bf16[2,128,2048]{2,1,0:T(8,128)(2,1)S(1)}, u32[]{:S(2)}, u32[]{:S(2)}) collective-permute-start(bf16[2,128,2048]{2,1,0:T(8,128)(2,1)S(1)} %pad_maximum_fusion.23), channel_id=1, source_target_pairs={{0,8},{1,9},{2,10},{3,11},{4,12},{5,13},{6,14},{7,15},{8,0},{9,1},... | collective-permute-start | bytes 3145736 | tf_op jit(solution)/shard_map/ppermute | solution.py:249
  538.2 22.5 %collective-permute-start.48 = (bf16[2,128,2048]{2,1,0:T(8,128)(2,1)S(1)}, bf16[2,128,2048]{2,1,0:T(8,128)(2,1)S(1)}, u32[]{:S(2)}, u32[]{:S(2)}) collective-permute-start(bf16[2,128,2048]{2,1,0:T(8,128)(2,1)S(1)} %pad_maximum_fusion.22), channel_id=1, source_target_pairs={{0,8},{1,9},{2,10},{3,11},{4,12},{5,13},{6,14},{7,15},{8,0},{9,1},... | collective-permute-start | bytes 3145736 | tf_op jit(solution)/shard_map/ppermute | solution.py:249
  539.0 24.3 %collective-permute-start.56 = (bf16[128,1024]{1,0:T(8,128)(2,1)S(1)}, bf16[128,1024]{1,0:T(8,128)(2,1)S(1)}, u32[]{:S(2)}, u32[]{:S(2)}) collective-permute-start(bf16[128,1024]{1,0:T(8,128)(2,1)S(1)} %get-tuple-element.105), channel_id=1, source_target_pairs={{0,1},{1,0},{2,3},{3,2},{4,5},{5,4},{6,7},{7,6},{8,9},{9,8},{10,11... | collective-permute-start | bytes 786440 | tf_op jit(solution)/shard_map/ppermute | solution.py:249
  540.8 22.5 %collective-permute-start.57 = (bf16[128,1024]{1,0:T(8,128)(2,1)S(1)}, bf16[128,1024]{1,0:T(8,128)(2,1)S(1)}, u32[]{:S(2)}, u32[]{:S(2)}) collective-permute-start(bf16[128,1024]{1,0:T(8,128)(2,1)S(1)} %get-tuple-element.106), channel_id=1, source_target_pairs={{0,4},{1,5},{2,6},{3,7},{4,0},{5,1},{6,2},{7,3},{8,12},{9,13},{10,... | collective-permute-start | bytes 786440 | tf_op jit(solution)/shard_map/ppermute | solution.py:249
  541.6 22.9 %collective-permute-start.32 = (bf16[128,1024]{1,0:T(8,128)(2,1)S(1)}, bf16[128,1024]{1,0:T(8,128)(2,1)S(1)}, u32[]{:S(2)}, u32[]{:S(2)}) collective-permute-start(bf16[128,1024]{1,0:T(8,128)(2,1)S(1)} %get-tuple-element.113), channel_id=1, source_target_pairs={{0,1},{1,0},{2,3},{3,2},{4,5},{5,4},{6,7},{7,6},{8,9},{9,8},{10,11... | collective-permute-start | bytes 786440 | tf_op jit(solution)/shard_map/ppermute | solution.py:249
  543.0 21.6 %collective-permute-start.33 = (bf16[128,1024]{1,0:T(8,128)(2,1)S(1)}, bf16[128,1024]{1,0:T(8,128)(2,1)S(1)}, u32[]{:S(2)}, u32[]{:S(2)}) collective-permute-start(bf16[128,1024]{1,0:T(8,128)(2,1)S(1)} %get-tuple-element.114), channel_id=1, source_target_pairs={{0,4},{1,5},{2,6},{3,7},{4,0},{5,1},{6,2},{7,3},{8,12},{9,13},{10,... | collective-permute-start | bytes 786440 | tf_op jit(solution)/shard_map/ppermute | solution.py:249
  563.4 22.4 %collective-permute-start.58 = (bf16[64,2048]{1,0:T(8,128)(2,1)S(1)}, bf16[64,2048]{1,0:T(8,128)(2,1)S(1)}, u32[]{:S(2)}, u32[]{:S(2)}) collective-permute-start(bf16[64,2048]{1,0:T(8,128)(2,1)S(1)} %pad_maximum_fusion.39), channel_id=1, source_target_pairs={{0,16},{1,17},{2,18},{3,19},{4,20},{5,21},{6,22},{7,23},{8,24},{9,... | collective-permute-start | bytes 786440 | tf_op jit(solution)/shard_map/ppermute | solution.py:249
  564.7 26.7 %collective-permute-start.34 = (bf16[64,2048]{1,0:T(8,128)(2,1)S(1)}, bf16[64,2048]{1,0:T(8,128)(2,1)S(1)}, u32[]{:S(2)}, u32[]{:S(2)}) collective-permute-start(bf16[64,2048]{1,0:T(8,128)(2,1)S(1)} %pad_maximum_fusion.41), channel_id=1, source_target_pairs={{0,16},{1,17},{2,18},{3,19},{4,20},{5,21},{6,22},{7,23},{8,24},{9,... | collective-permute-start | bytes 786440 | tf_op jit(solution)/shard_map/ppermute | solution.py:249
  570.5 26.5 %collective-permute-start.51 = (bf16[64,2048]{1,0:T(8,128)(2,1)}, bf16[64,2048]{1,0:T(8,128)(2,1)S(1)}, u32[]{:S(2)}, u32[]{:S(2)}) collective-permute-start(bf16[64,2048]{1,0:T(8,128)(2,1)} %pad_maximum_fusion.40), channel_id=1, source_target_pairs={{0,16},{1,17},{2,18},{3,19},{4,20},{5,21},{6,22},{7,23},{8,24},{9,... | collective-permute-start | bytes 786440 | tf_op jit(solution)/shard_map/ppermute | solution.py:249
  (115 other events, 2169.3 us)
